TPU v7x, 32 devices: a whole 2x2x4 slice. The times are simulated.
32 devices in a mesh: tensor: 4 (over x, core), seq: 4 (over z), dp: 2 (over y).
Axes of the slice: x: 2, y: 2, z: 4, core: 2. Of those that a mesh axis runs over, the one named last changes fastest.
Arguments:
- inputs: bfloat16 [2, 1024, 768], P('dp', 'seq'), may hold values from -6 to 6
- cotangent: float32 [2, 1024, 768], P('dp', 'seq'), may hold values from -6 to 6
- attention_norm_gain: float32 [2, 768], replicated, may hold values from 0.1 to 1.9
- attention_norm_bias: float32 [2, 768], replicated, may hold values from -3 to 3
- w_query: bfloat16 [2, 768, 768], P(None, ('seq', 'dp'), 'tensor'), may hold values from -0.21875 to 0.21875
- b_query: float32 [2, 768], P(None, 'tensor'), may hold values from -3 to 3
- w_key: bfloat16 [2, 768, 768], P(None, ('seq', 'dp'), 'tensor'), may hold values from -0.21875 to 0.21875
- w_value: bfloat16 [2, 768, 768], P(None, ('seq', 'dp'), 'tensor'), may hold values from -0.21875 to 0.21875
- b_value: float32 [2, 768], P(None, 'tensor'), may hold values from -0.6 to 0.6
- w_out: bfloat16 [2, 768, 768], P(None, ('seq', 'dp'), 'tensor'), may hold values from -0.875 to 0.875
- b_out: float32 [2, 768], replicated, may hold values from -3 to 3
- feedforward_norm_gain: float32 [2, 768], replicated, may hold values from 0.1 to 1.9
- feedforward_norm_bias: float32 [2, 768], replicated, may hold values from -3 to 3
- w_fc1: bfloat16 [2, 768, 3072], P(None, ('seq', 'dp'), 'tensor'), may hold values from -0.21875 to 0.21875
- b_fc1: float32 [2, 3072], P(None, 'tensor'), may hold values from -3 to 3
- w_fc2: bfloat16 [2, 768, 3072], P(None, ('seq', 'dp'), 'tensor'), may hold values from -0.109375 to 0.109375
- b_fc2: float32 [2, 768], replicated, may hold values from -3 to 3
Outputs:
- encoded: float32 [2, 1024, 768], P('dp', 'seq')
- grad_inputs: float32 [2, 1024, 768], P('dp', 'seq')
- grad_ln1_gain: float32 [2, 768], replicated
- grad_ln1_bias: float32 [2, 768], replicated
- grad_w_query: float32 [2, 768, 768], P(None, ('seq', 'dp'), 'tensor')
- grad_b_query: float32 [2, 768], P(None, 'tensor')
- grad_w_key: float32 [2, 768, 768], P(None, ('seq', 'dp'), 'tensor')
- grad_w_value: float32 [2, 768, 768], P(None, ('seq', 'dp'), 'tensor')
- grad_b_value: float32 [2, 768], P(None, 'tensor')
- grad_w_out: float32 [2, 768, 768], P(None, ('seq', 'dp'), 'tensor')
- grad_b_out: float32 [2, 768], replicated
- grad_ln2_gain: float32 [2, 768], replicated
- grad_ln2_bias: float32 [2, 768], replicated
- grad_w_fc1: float32 [2, 768, 3072], P(None, ('seq', 'dp'), 'tensor')
- grad_b_fc1: float32 [2, 3072], P(None, 'tensor')
- grad_w_fc2: float32 [2, 768, 3072], P(None, ('seq', 'dp'), 'tensor')
- grad_b_fc2: float32 [2, 768], replicated
All inputs are finite; a program needn't handle non-finite values.
Results may differ from a plain program's by a relative error of at most 0.029.
Values may be sent and summed in bfloat16 or wider, within the bound.
A program may use at most 128 MiB of HBM per device.

v0:
```python
import math

import jax
import jax.numpy as jnp
from jax import lax
from jax.sharding import PartitionSpec as P

HEAD_DIM = 64


EPSILON = 1e-05
INV_ROOT_TWO = 1.0 / math.sqrt(2.0)
INV_ROOT_TWO_PI = 1.0 / math.sqrt(2.0 * math.pi)


def standardize_rows(values):
    center = values - jnp.mean(values, -1, keepdims=True)
    inverse_scale = lax.rsqrt(jnp.mean(center * center, -1, keepdims=True) + EPSILON)
    return (center * inverse_scale, inverse_scale)


def norm_backward_pass(output_gradient, centered_normalized, inverse_scale, norm_gain):
    scaled_values = output_gradient * norm_gain
    return inverse_scale * (
        scaled_values
        - jnp.mean(scaled_values, -1, keepdims=True)
        - centered_normalized * jnp.mean(scaled_values * centered_normalized, -1, keepdims=True)
    )


def times_trans(left, right):
    return lax.dot_general(
        left, right, (((1,), (1,)), ((), ())), preferred_element_type=jnp.float32
    )


def trans_times(left, right):
    return lax.dot_general(
        left, right, (((0,), (0,)), ((), ())), preferred_element_type=jnp.float32
    )


def matmul(left, right):
    return jnp.dot(left, right, preferred_element_type=jnp.float32)


def gelu_slope(pre_act):
    return (
        0.5 * (1.0 + jax.scipy.special.erf(pre_act * INV_ROOT_TWO))
        + pre_act * jnp.exp(-0.5 * pre_act * pre_act) * INV_ROOT_TWO_PI
    )


def split_heads(block):
    return block.reshape(block.shape[0], block.shape[1] // HEAD_DIM, HEAD_DIM)


def attend_forward(pieces):
    query_blk, key_blk, value_blk = pieces
    scale = HEAD_DIM ** (-0.5)
    scores = (
        jnp.einsum(
            "qhd,khd->hqk",
            split_heads(query_blk),
            split_heads(key_blk),
            preferred_element_type=jnp.float32,
        )
        * scale
    )
    top = jnp.max(scores, -1, keepdims=True)
    expo = jnp.exp(scores - top)
    total = jnp.sum(expo, -1, keepdims=True)
    prob = (expo / total).astype(jnp.bfloat16)
    attended = jnp.einsum(
        "hqk,khd->qhd", prob, split_heads(value_blk), preferred_element_type=jnp.float32
    )
    attended = attended.reshape(query_blk.shape[0], -1).astype(jnp.bfloat16)
    return (attended, (top + jnp.log(total))[..., 0])


def score_grads(query_heads, key_heads, value_heads, log_total, grad_heads, inner):
    scale = HEAD_DIM ** (-0.5)
    scores = (
        jnp.einsum("qhd,khd->hqk", query_heads, key_heads, preferred_element_type=jnp.float32)
        * scale
    )
    prob = jnp.exp(scores - log_total[..., None])
    grad_prob = jnp.einsum(
        "qhd,khd->hqk", grad_heads, value_heads, preferred_element_type=jnp.float32
    )
    inner = jnp.sum(prob * grad_prob, -1)
    grad_scores = (prob * (grad_prob - inner[..., None])).astype(jnp.bfloat16)
    return (prob, grad_scores, inner)


def key_side(grad_scores, prob, query_heads, grad_heads, frames_all):
    scale = HEAD_DIM ** (-0.5)
    grad_key = (
        jnp.einsum("hqk,qhd->khd", grad_scores, query_heads, preferred_element_type=jnp.float32)
        * scale
    )
    grad_value = jnp.einsum(
        "hqk,qhd->khd", prob.astype(jnp.bfloat16), grad_heads, preferred_element_type=jnp.float32
    )
    return jnp.concatenate(
        [grad_key.reshape(frames_all, -1), grad_value.reshape(frames_all, -1)], 1
    )


def attend_backward(pieces):
    query_blk, key_blk, value_blk, log_total, grad_blk = pieces
    query_heads = split_heads(query_blk)
    key_heads = split_heads(key_blk)
    grad_heads = split_heads(grad_blk)
    prob, grad_scores, inner = score_grads(
        query_heads, key_heads, split_heads(value_blk), log_total, grad_heads, None
    )
    grad_query = jnp.einsum(
        "hqk,khd->qhd", grad_scores, key_heads, preferred_element_type=jnp.float32
    ) * HEAD_DIM ** (-0.5)
    joined = key_side(grad_scores, prob, query_heads, grad_heads, key_blk.shape[0])
    return (grad_query.reshape(query_blk.shape[0], -1), joined)


def branch_total(partial_value):
    share = lax.psum_scatter(
        partial_value.astype(jnp.bfloat16), "tensor", scatter_dimension=0, tiled=True
    ).astype(jnp.float32)
    return lax.all_gather(share.astype(jnp.bfloat16), "tensor", axis=0, tiled=True).astype(
        share.dtype
    )


def norm_total(partial_value):
    share = lax.psum_scatter(
        partial_value.astype(jnp.bfloat16), "tensor", scatter_dimension=0, tiled=True
    ).astype(jnp.float32)
    return lax.all_gather(share.astype(jnp.bfloat16), "tensor", axis=0, tiled=True).astype(
        share.dtype
    )


def per_device(
    inputs,
    cotangent,
    attention_norm_gain,
    attention_norm_bias,
    w_query,
    b_query,
    w_key,
    w_value,
    b_value,
    w_out,
    b_out,
    feedforward_norm_gain,
    feedforward_norm_bias,
    w_fc1,
    b_fc1,
    w_fc2,
    b_fc2,
):
    clips, frames_local, width = inputs.shape
    rows = clips * frames_local
    layers = w_query.shape[0]
    piece_rows = width // lax.axis_size(("seq", "dp"))
    cols_heads = w_query.shape[2]
    cols_hidden = w_fc1.shape[2]
    hidden_state = inputs.astype(jnp.float32).reshape(rows, width)
    kept_mats = []
    saved_all = []
    for layer_params in range(layers):
        mats = (
            lax.all_gather(w_query[layer_params], ("seq", "dp"), axis=0, tiled=True),
            lax.all_gather(w_key[layer_params], ("seq", "dp"), axis=0, tiled=True),
            lax.all_gather(w_value[layer_params], ("seq", "dp"), axis=0, tiled=True),
            lax.all_gather(w_out[layer_params], ("seq", "dp"), axis=0, tiled=True),
            lax.all_gather(w_fc1[layer_params], ("seq", "dp"), axis=0, tiled=True),
            lax.all_gather(w_fc2[layer_params], ("seq", "dp"), axis=0, tiled=True),
        )
        full_q, full_k, full_v, full_o, full_up, full_down = mats
        first_centered_normalized, first_inverse_deviation = standardize_rows(hidden_state)
        normalized_input = (
            first_centered_normalized * attention_norm_gain[layer_params]
            + attention_norm_bias[layer_params]
        ).astype(jnp.bfloat16)
        queries = (
            (matmul(normalized_input, full_q) + b_query[layer_params])
            .astype(jnp.bfloat16)
            .reshape(clips, frames_local, cols_heads)
        )
        keys_local = (
            matmul(normalized_input, full_k)
            .astype(jnp.bfloat16)
            .reshape(clips, frames_local, cols_heads)
        )
        values_local = (
            (matmul(normalized_input, full_v) + b_value[layer_params])
            .astype(jnp.bfloat16)
            .reshape(clips, frames_local, cols_heads)
        )
        keys_all, values_all = (
            lax.all_gather(keys_local, "seq", axis=1, tiled=True),
            lax.all_gather(values_local, "seq", axis=1, tiled=True),
        )
        attended, log_total = lax.map(attend_forward, (queries, keys_all, values_all))
        attended = attended.reshape(rows, cols_heads)
        middle_state = hidden_state + (
            branch_total(times_trans(attended, full_o)) + b_out[layer_params]
        )
        second_centered_normalized, second_inverse_deviation = standardize_rows(middle_state)
        second_normalized = (
            second_centered_normalized * feedforward_norm_gain[layer_params]
            + feedforward_norm_bias[layer_params]
        ).astype(jnp.bfloat16)
        pre_act = matmul(second_normalized, full_up) + b_fc1[layer_params]
        activated = jax.nn.gelu(pre_act, approximate=False).astype(jnp.bfloat16)
        hidden_state = middle_state + (
            branch_total(times_trans(activated, full_down)) + b_fc2[layer_params]
        )
        kept_mats.append(mats)
        saved_all.append(
            (
                first_centered_normalized,
                first_inverse_deviation,
                normalized_input,
                queries,
                keys_local,
                values_local,
                keys_all,
                values_all,
                log_total,
                attended,
                second_centered_normalized,
                second_inverse_deviation,
                second_normalized,
                pre_act,
                activated,
            )
        )
    encoded = hidden_state.reshape(clips, frames_local, width)
    state_gradient = cotangent.reshape(rows, width)
    big_grads = [None] * layers
    small_all = [None] * layers
    for layer_params in reversed(range(layers)):
        mats = (
            lax.all_gather(w_query[layer_params], ("seq", "dp"), axis=0, tiled=True),
            lax.all_gather(w_key[layer_params], ("seq", "dp"), axis=0, tiled=True),
            lax.all_gather(w_value[layer_params], ("seq", "dp"), axis=0, tiled=True),
            lax.all_gather(w_out[layer_params], ("seq", "dp"), axis=0, tiled=True),
            lax.all_gather(w_fc1[layer_params], ("seq", "dp"), axis=0, tiled=True),
            lax.all_gather(w_fc2[layer_params], ("seq", "dp"), axis=0, tiled=True),
        )
        full_q, full_k, full_v, full_o, full_up, full_down = mats
        (
            first_centered_normalized,
            first_inverse_deviation,
            normalized_input,
            queries,
            keys_local,
            values_local,
            keys_all,
            values_all,
            log_total,
            attended,
            second_centered_normalized,
            second_inverse_deviation,
            second_normalized,
            pre_act,
            activated,
        ) = saved_all[layer_params]
        grad_mlp = state_gradient.astype(jnp.bfloat16)
        grad_pre = (matmul(grad_mlp, full_down) * gelu_slope(pre_act)).astype(jnp.bfloat16)
        second_norm_gradient = norm_total(times_trans(grad_pre, full_up))
        middle_gradient = state_gradient + norm_backward_pass(
            second_norm_gradient,
            second_centered_normalized,
            second_inverse_deviation,
            feedforward_norm_gain[layer_params],
        )
        grad_attn = middle_gradient.astype(jnp.bfloat16)
        grad_attended = (
            matmul(grad_attn, full_o).astype(jnp.bfloat16).reshape(clips, frames_local, cols_heads)
        )
        grad_query, kv_terms = lax.map(
            attend_backward, (queries, keys_all, values_all, log_total, grad_attended)
        )
        kv_grads = lax.psum_scatter(
            kv_terms.astype(jnp.bfloat16), "seq", scatter_dimension=1, tiled=True
        )
        grad_query = grad_query.reshape(rows, cols_heads).astype(jnp.bfloat16)
        grad_key = kv_grads[:, :, :cols_heads].reshape(rows, cols_heads)
        grad_value = kv_grads[:, :, cols_heads:].reshape(rows, cols_heads)
        first_norm_gradient = norm_total(
            times_trans(grad_query, full_q)
            + times_trans(grad_key, full_k)
            + times_trans(grad_value, full_v)
        )
        state_gradient = middle_gradient + norm_backward_pass(
            first_norm_gradient,
            first_centered_normalized,
            first_inverse_deviation,
            attention_norm_gain[layer_params],
        )

        def weight_terms(
            start,
            count,
            normalized_input=normalized_input,
            grad_query=grad_query,
            grad_key=grad_key,
            grad_value=grad_value,
            grad_attn=grad_attn,
            attended=attended,
            second_normalized=second_normalized,
            grad_pre=grad_pre,
            grad_mlp=grad_mlp,
            activated=activated,
        ):
            return jnp.concatenate(
                [
                    trans_times(normalized_input, grad_query),
                    trans_times(normalized_input, grad_key),
                    trans_times(normalized_input, grad_value),
                    trans_times(grad_attn, attended),
                    trans_times(second_normalized, grad_pre),
                    trans_times(grad_mlp, activated),
                ],
                1,
            )

        big_grads[layer_params] = lax.psum_scatter(
            weight_terms(jnp.int32(0), lax.axis_size(("seq", "dp")) * piece_rows),
            ("seq", "dp"),
            scatter_dimension=0,
            tiled=True,
        )
        small_all[layer_params] = lax.psum(
            (
                jnp.sum(first_norm_gradient * first_centered_normalized, 0),
                jnp.sum(first_norm_gradient, 0),
                jnp.sum(grad_query, 0, dtype=jnp.float32),
                jnp.sum(grad_value, 0, dtype=jnp.float32),
                jnp.sum(grad_attn, 0, dtype=jnp.float32),
                jnp.sum(second_norm_gradient * second_centered_normalized, 0),
                jnp.sum(second_norm_gradient, 0),
                jnp.sum(grad_pre, 0, dtype=jnp.float32),
                jnp.sum(grad_mlp, 0, dtype=jnp.float32),
            ),
            ("seq", "dp"),
        )
    stacked = jnp.stack(big_grads, 0)
    edges = [
        0,
        cols_heads,
        2 * cols_heads,
        3 * cols_heads,
        4 * cols_heads,
        4 * cols_heads + cols_hidden,
        4 * cols_heads + 2 * cols_hidden,
    ]
    grad_w_query = stacked[:, :, edges[0] : edges[1]]
    grad_w_key = stacked[:, :, edges[1] : edges[2]]
    grad_w_value = stacked[:, :, edges[2] : edges[3]]
    grad_w_out = stacked[:, :, edges[3] : edges[4]]
    grad_w_fc1 = stacked[:, :, edges[4] : edges[5]]
    grad_w_fc2 = stacked[:, :, edges[5] : edges[6]]
    small_stack = [
        jnp.stack([small_all[layer_params][member] for layer_params in range(layers)], 0)
        for member in range(9)
    ]
    grad_inputs = state_gradient.reshape(clips, frames_local, width)
    return (
        encoded,
        grad_inputs,
        small_stack[0],
        small_stack[1],
        grad_w_query,
        small_stack[2],
        grad_w_key,
        grad_w_value,
        small_stack[3],
        grad_w_out,
        small_stack[4],
        small_stack[5],
        small_stack[6],
        grad_w_fc1,
        small_stack[7],
        grad_w_fc2,
        small_stack[8],
    )


def solution(mesh):
    placed = (
        P("dp", "seq", None),
        P("dp", "seq", None),
        P(),
        P(),
        P(None, ("seq", "dp"), "tensor"),
        P(None, "tensor"),
        P(None, ("seq", "dp"), "tensor"),
        P(None, ("seq", "dp"), "tensor"),
        P(None, "tensor"),
        P(None, ("seq", "dp"), "tensor"),
        P(),
        P(),
        P(),
        P(None, ("seq", "dp"), "tensor"),
        P(None, "tensor"),
        P(None, ("seq", "dp"), "tensor"),
        P(),
    )
    return jax.shard_map(
        per_device,
        mesh=mesh,
        in_specs=placed,
        out_specs=(
            P("dp", "seq", None),
            P("dp", "seq", None),
            P(),
            P(),
            P(None, ("seq", "dp"), "tensor"),
            P(None, "tensor"),
            P(None, ("seq", "dp"), "tensor"),
            P(None, ("seq", "dp"), "tensor"),
            P(None, "tensor"),
            P(None, ("seq", "dp"), "tensor"),
            P(),
            P(),
            P(),
            P(None, ("seq", "dp"), "tensor"),
            P(None, "tensor"),
            P(None, ("seq", "dp"), "tensor"),
            P(),
        ),
        check_vma=False,
    )
```

profile of v0, /device:TPU:0, one launch (start us, length us, event | category | flops | bytes accessed | tf_op | source)
XLA Modules:
  0.0 1035.1 jit_solution(15439816998085848417)
XLA Ops:
  14.2 32.7 %all-gather.2 = bf16[1,768,192]{2,1,0:T(8,128)(2,1)S(1)} all-gather(bf16[1,96,192]{2,1,0:T(8,128)(2,1)S(1)} %get-tuple-element.210), channel_id=4, replica_groups=mesh['tensor'=4,'seq'=4,'dp'=2] {'seq','dp'}, dimensions={1}, use_global_device_ids=true | all-gather | bytes 331776 | tf_op jit(solution)/shard_map/all_gather | solution.py:173
  49.7 31.1 %all-gather.3 = bf16[1,768,192]{2,1,0:T(8,128)(2,1)S(1)} all-gather(bf16[1,96,192]{2,1,0:T(8,128)(2,1)S(1)} %get-tuple-element.208), channel_id=5, replica_groups=mesh['tensor'=4,'seq'=4,'dp'=2] {'seq','dp'}, dimensions={1}, use_global_device_ids=true | all-gather | bytes 331776 | tf_op jit(solution)/shard_map/all_gather | solution.py:174
  82.4 14.6 %all-gather.4 = bf16[1024,192]{0,1:T(8,128)(2,1)S(1)} all-gather(bf16[256,192]{0,1:T(8,128)(2,1)S(1)} %convolution_convert_fusion.9), channel_id=6, replica_groups=mesh['tensor'=4,'seq'=4,'dp'=2] {'seq'}, dimensions={0}, use_global_device_ids=true | all-gather | bytes 491520 | tf_op jit(solution)/shard_map/all_gather | solution.py:202
  97.8 31.3 %all-gather = bf16[1,768,192]{2,1,0:T(8,128)(2,1)S(1)} all-gather(bf16[1,96,192]{2,1,0:T(8,128)(2,1)S(1)} %get-tuple-element.212), channel_id=2, replica_groups=mesh['tensor'=4,'seq'=4,'dp'=2] {'seq','dp'}, dimensions={1}, use_global_device_ids=true | all-gather | bytes 331776 | tf_op jit(solution)/shard_map/all_gather | solution.py:175
  130.1 14.4 %all-gather.1 = bf16[1024,192]{0,1:T(8,128)(2,1)S(1)} all-gather(bf16[256,192]{0,1:T(8,128)(2,1)S(1)} %fusion.34), channel_id=3, replica_groups=mesh['tensor'=4,'seq'=4,'dp'=2] {'seq'}, dimensions={0}, use_global_device_ids=true | all-gather | bytes 491520 | tf_op jit(solution)/shard_map/all_gather | solution.py:203
  145.2 30.9 %all-gather.5 = bf16[1,768,192]{2,1,0:T(8,128)(2,1)S(1)} all-gather(bf16[1,96,192]{2,1,0:T(8,128)(2,1)S(1)} %get-tuple-element.206), channel_id=7, replica_groups=mesh['tensor'=4,'seq'=4,'dp'=2] {'seq','dp'}, dimensions={1}, use_global_device_ids=true | all-gather | bytes 331776 | tf_op jit(solution)/shard_map/all_gather | solution.py:176
  211.2 15.5 %all-gather.21.cloned.1.call-done = bf16[1,768,768]{2,1,0:T(8,128)(2,1)} async-done(((bf16[1,96,768]{2,1,0:T(8,128)(2,1)}), bf16[1,768,768]{2,1,0:T(8,128)(2,1)}) %all-gather.21.cloned.1.call-update) | async-done | bytes 1179664 | tf_op jit(solution)/shard_map/all_gather | solution.py:177
  229.6 39.8 %all-gather.23.cloned.1.call-done = bf16[1,768,768]{2,1,0:T(8,128)(2,1)} async-done(((bf16[1,96,768]{2,1,0:T(8,128)(2,1)}), bf16[1,768,768]{2,1,0:T(8,128)(2,1)}) %all-gather.23.cloned.1.call-update) | async-done | bytes 1179664 | tf_op jit(solution)/shard_map/all_gather | solution.py:178
  275.1 33.4 %all-gather.11 = bf16[1,768,192]{2,1,0:T(8,128)(2,1)} all-gather(bf16[1,96,192]{2,1,0:T(8,128)(2,1)} %get-tuple-element.207), channel_id=13, replica_groups=mesh['tensor'=4,'seq'=4,'dp'=2] {'seq','dp'}, dimensions={1}, use_global_device_ids=true | all-gather | bytes 331776 | tf_op jit(solution)/shard_map/all_gather | solution.py:174
  308.5 33.5 %all-gather.10 = bf16[1,768,192]{2,1,0:T(8,128)(2,1)} all-gather(bf16[1,96,192]{2,1,0:T(8,128)(2,1)} %get-tuple-element.209), channel_id=12, replica_groups=mesh['tensor'=4,'seq'=4,'dp'=2] {'seq','dp'}, dimensions={1}, use_global_device_ids=true | all-gather | bytes 331776 | tf_op jit(solution)/shard_map/all_gather | solution.py:173
  342.0 33.2 %all-gather.8 = bf16[1,768,192]{2,1,0:T(8,128)(2,1)} all-gather(bf16[1,96,192]{2,1,0:T(8,128)(2,1)} %get-tuple-element.211), channel_id=10, replica_groups=mesh['tensor'=4,'seq'=4,'dp'=2] {'seq','dp'}, dimensions={1}, use_global_device_ids=true | all-gather | bytes 331776 | tf_op jit(solution)/shard_map/all_gather | solution.py:175
  375.2 33.4 %all-gather.13 = bf16[1,768,192]{2,1,0:T(8,128)(2,1)} all-gather(bf16[1,96,192]{2,1,0:T(8,128)(2,1)} %get-tuple-element.205), channel_id=15, replica_groups=mesh['tensor'=4,'seq'=4,'dp'=2] {'seq','dp'}, dimensions={1}, use_global_device_ids=true | all-gather | bytes 331776 | tf_op jit(solution)/shard_map/all_gather | solution.py:176
  417.6 15.3 %all-gather.12 = bf16[1024,192]{0,1:T(8,128)(2,1)S(1)} all-gather(bf16[256,192]{0,1:T(8,128)(2,1)S(1)} %convolution_convert_fusion.8), channel_id=14, replica_groups=mesh['tensor'=4,'seq'=4,'dp'=2] {'seq'}, dimensions={0}, use_global_device_ids=true | all-gather | bytes 491520 | tf_op jit(solution)/shard_map/all_gather | solution.py:202
  433.2 14.6 %all-gather.9 = bf16[1024,192]{0,1:T(8,128)(2,1)S(1)} all-gather(bf16[256,192]{0,1:T(8,128)(2,1)S(1)} %fusion.36), channel_id=11, replica_groups=mesh['tensor'=4,'seq'=4,'dp'=2] {'seq'}, dimensions={0}, use_global_device_ids=true | all-gather | bytes 491520 | tf_op jit(solution)/shard_map/all_gather | solution.py:203
  453.7 17.5 %reduce-scatter.21.cloned.1.call-done = bf16[64,768]{1,0:T(8,128)(2,1)} async-done(((bf16[256,768]{1,0:T(8,128)(2,1)}), bf16[64,768]{1,0:T(8,128)(2,1)}) %reduce-scatter.21.cloned.1.call-update) | async-done | bytes 98320 | tf_op jit(solution)/shard_map/reduce_scatter | solution.py:126
  480.5 14.4 %all-gather.25.cloned.1.call-done = bf16[1,768,768]{2,1,0:T(8,128)(2,1)} async-done(((bf16[1,96,768]{2,1,0:T(8,128)(2,1)}), bf16[1,768,768]{2,1,0:T(8,128)(2,1)}) %all-gather.25.cloned.1.call-update) | async-done | bytes 1179664 | tf_op jit(solution)/shard_map/all_gather | solution.py:177
  497.9 39.9 %all-gather.27.cloned.1.call-done = bf16[1,768,768]{2,1,0:T(8,128)(2,1)} async-done(((bf16[1,96,768]{2,1,0:T(8,128)(2,1)}), bf16[1,768,768]{2,1,0:T(8,128)(2,1)}) %all-gather.27.cloned.1.call-update) | async-done | bytes 1179664 | tf_op jit(solution)/shard_map/all_gather | solution.py:178
  607.2 17.9 %reduce-scatter.27.cloned.1.call-done = bf16[1,256,384]{1,2,0:T(8,128)(2,1)} async-done(((bf16[1,1024,384]{1,2,0:T(8,128)(2,1)}), bf16[1,256,384]{1,2,0:T(8,128)(2,1)}) %reduce-scatter.27.cloned.1.call-update) | async-done | bytes 196624 | tf_op jit(solution)/shard_map/reduce_scatter | solution.py:287
  628.9 20.2 %reduce-scatter.29.cloned.1.call-done = bf16[64,768]{1,0:T(8,128)(2,1)} async-done(((bf16[256,768]{1,0:T(8,128)(2,1)}), bf16[64,768]{1,0:T(8,128)(2,1)}) %reduce-scatter.29.cloned.1.call-update) | async-done | bytes 98320 | tf_op jit(solution)/shard_map/reduce_scatter | solution.py:135
  665.0 20.6 %reduce-scatter.31.cloned.1.call-done = bf16[64,768]{1,0:T(8,128)(2,1)} async-done(((bf16[256,768]{1,0:T(8,128)(2,1)}), bf16[64,768]{1,0:T(8,128)(2,1)}) %reduce-scatter.31.cloned.1.call-update) | async-done | bytes 98320 | tf_op jit(solution)/shard_map/reduce_scatter | solution.py:135
  711.6 14.5 %reduce-scatter.33.cloned.1.call-done = bf16[1,256,384]{1,2,0:T(8,128)(2,1)} async-done(((bf16[1,1024,384]{1,2,0:T(8,128)(2,1)}), bf16[1,256,384]{1,2,0:T(8,128)(2,1)}) %reduce-scatter.33.cloned.1.call-update) | async-done | bytes 196624 | tf_op jit(solution)/shard_map/reduce_scatter | solution.py:287
  772.4 38.7 %all-reduce = (f32[1,768]{1,0:T(1,128)S(1)}, f32[1,768]{1,0:T(1,128)S(1)}, f32[1,768]{1,0:T(1,128)S(1)}, f32[1,768]{1,0:T(1,128)S(1)}, f32[1,192]{1,0:T(1,128)S(...) all-reduce(f32[1,768]{1,0:T(1,128)S(1)} %stack.91, ...), channel_id=1, replica_groups=mesh['tensor'=4,'seq'=4,'dp'=2] {'seq','dp'}, use_global_device_ids=true, to_apply=%region_35.36 | all-reduce | flops 11520 | bytes 92160 | tf_op jit(solution)/shard_map/psum | solution.py:337
  817.7 66.5 %reduce-scatter.39.cloned.1.call-done = f32[96,2304]{1,0:T(8,128)} async-done(((f32[768,2304]{1,0:T(8,128)}), f32[96,2304]{1,0:T(8,128)}) %reduce-scatter.39.cloned.1.call-update) | async-done | bytes 884752
  885.7 130.5 %reduce-scatter.37.cloned.1.call-done = f32[96,2304]{1,0:T(8,128)} async-done(((f32[768,2304]{1,0:T(8,128)}), f32[96,2304]{1,0:T(8,128)}) %reduce-scatter.37.cloned.1.call-update) | async-done | bytes 884752
  (397 shorter events, 263.3 us)
Async XLA Ops:
  8.0 121.6 %copy-start.2 = (bf16[1,256,768]{2,1,0:T(8,128)(2,1)S(1)}, bf16[1,256,768]{2,1,0:T(8,128)(2,1)}, u32[]{:S(2)}) copy-start(bf16[1,256,768]{2,1,0:T(8,128)(2,1)} %param.17) | copy-start | bytes 1179652
  8.0 121.0 %copy-start.100 = (f32[2,192]{1,0:T(2,128)S(1)}, f32[2,192]{1,0:T(2,128)}, u32[]{:S(2)}) copy-start(f32[2,192]{1,0:T(2,128)} %param.25) | copy-start | bytes 4612
  8.1 194.9 %reduce-scatter.17.cloned.1.call-start = ((), (), s32[]{:S(2)}) async-start(), calls=%async_computation.12 | async-start | bytes 491520 | tf_op jit(solution)/shard_map/reduce_scatter | solution.py:126
  9.3 135.3 %copy-start.61 = (bf16[2,96,192]{2,1,0:T(8,128)(2,1)S(1)}, bf16[2,96,192]{2,1,0:T(8,128)(2,1)}, u32[]{:S(2)}) copy-start(bf16[2,96,192]{2,1,0:T(8,128)(2,1)} %param.26) | copy-start | bytes 221188
  9.3 166.8 %copy-start.72 = (f32[256]{0:T(256)}, f32[256]{0:T(256)S(1)}, u32[]{:S(2)}) copy-start(f32[256]{0:T(256)S(1)} %broadcast_multiply_fusion.11) | copy-start | bytes 3076
  10.6 165.6 %copy-start.90 = (f32[256]{0:T(256)}, f32[256]{0:T(256)S(1)}, u32[]{:S(2)}) copy-start(f32[256]{0:T(256)S(1)} %add_rsqrt_fusion.3) | copy-start | bytes 3076
  11.4 164.8 %copy-start.63 = (f32[768]{0:T(1024)}, f32[768]{0:T(1024)S(1)}, u32[]{:S(2)}) copy-start(f32[768]{0:T(1024)S(1)} %get-tuple-element.162) | copy-start | bytes 9220
  12.8 163.4 %copy-start.94 = (f32[768]{0:T(1024)}, f32[768]{0:T(1024)S(1)}, u32[]{:S(2)}) copy-start(f32[768]{0:T(1024)S(1)} %get-tuple-element.164) | copy-start | bytes 9220
  47.0 129.6 %copy-start.34 = (bf16[1,768,192]{2,1,0:T(8,128)(2,1)}, bf16[1,768,192]{2,1,0:T(8,128)(2,1)S(1)}, u32[]{:S(2)}) copy-start(bf16[1,768,192]{2,1,0:T(8,128)(2,1)S(1)} %all-gather.2) | copy-start | bytes 884740
  180.7 46.1 %all-gather.21.cloned.1.call-start = ((), (), s32[]{:S(2)}) async-start(), calls=%async_computation.22 | async-start | bytes 1327104 | tf_op jit(solution)/shard_map/all_gather | solution.py:177
  182.4 86.9 %all-gather.23.cloned.1.call-start = ((), (), s32[]{:S(2)}) async-start(), calls=%async_computation.23 | async-start | bytes 1327104 | tf_op jit(solution)/shard_map/all_gather | solution.py:178
  184.2 224.3 %reduce-scatter.19.cloned.1.call-start = ((), (), s32[]{:S(2)}) async-start(), calls=%async_computation.13 | async-start | bytes 491520 | tf_op jit(solution)/shard_map/reduce_scatter | solution.py:126
  273.7 197.4 %reduce-scatter.21.cloned.1.call-start = ((), (), s32[]{:S(2)}) async-start(), calls=%async_computation.14 | async-start | bytes 491520 | tf_op jit(solution)/shard_map/reduce_scatter | solution.py:126
  452.3 42.6 %all-gather.25.cloned.1.call-start = ((), (), s32[]{:S(2)}) async-start(), calls=%async_computation.24 | async-start | bytes 1327104 | tf_op jit(solution)/shard_map/all_gather | solution.py:177
  452.9 84.8 %all-gather.27.cloned.1.call-start = ((), (), s32[]{:S(2)}) async-start(), calls=%async_computation.25 | async-start | bytes 1327104 | tf_op jit(solution)/shard_map/all_gather | solution.py:178
  453.6 108.6 %reduce-scatter.25.cloned.1.call-start = ((), (), s32[]{:S(2)}) async-start(), calls=%async_computation.16 | async-start | bytes 491520 | tf_op jit(solution)/shard_map/reduce_scatter | solution.py:135
  542.8 43.3 %reduce-scatter.23.cloned.1.call-start = ((), (), s32[]{:S(2)}) async-start(), calls=%async_computation.15 | async-start | bytes 491520 | tf_op jit(solution)/shard_map/reduce_scatter | solution.py:126
  547.1 77.9 %reduce-scatter.27.cloned.1.call-start = ((), (), s32[]{:S(2)}) async-start(), calls=%async_computation.17 | async-start | bytes 983040 | tf_op jit(solution)/shard_map/reduce_scatter | solution.py:287
  601.3 47.8 %reduce-scatter.29.cloned.1.call-start = ((), (), s32[]{:S(2)}) async-start(), calls=%async_computation.18 | async-start | bytes 491520 | tf_op jit(solution)/shard_map/reduce_scatter | solution.py:135
  628.8 56.7 %reduce-scatter.31.cloned.1.call-start = ((), (), s32[]{:S(2)}) async-start(), calls=%async_computation.19 | async-start | bytes 491520 | tf_op jit(solution)/shard_map/reduce_scatter | solution.py:135
  664.2 61.9 %reduce-scatter.33.cloned.1.call-start = ((), (), s32[]{:S(2)}) async-start(), calls=%async_computation.20 | async-start | bytes 983040 | tf_op jit(solution)/shard_map/reduce_scatter | solution.py:287
  702.4 62.8 %reduce-scatter.35.cloned.1.call-start = ((), (), s32[]{:S(2)}) async-start(), calls=%async_computation.21 | async-start | bytes 491520 | tf_op jit(solution)/shard_map/reduce_scatter | solution.py:135
  729.6 154.6 %reduce-scatter.39.cloned.1.call-start = ((), (), s32[]{:S(2)}) async-start(), calls=%async_computation.27 | async-start | bytes 7962624
  744.4 271.8 %reduce-scatter.37.cloned.1.call-start = ((), (), s32[]{:S(2)}) async-start(), calls=%async_computation.26 | async-start | bytes 7962624
  (97 other events, 941.2 us)
Sparse Core Ops, SparseCore 0:
  180.8 22.1 reduce-scatter.16
  273.8 19.3 reduce-scatter.18
  452.4 18.6 reduce-scatter.20
  542.9 19.3 reduce-scatter.24
  565.1 20.8 reduce-scatter.22
  601.4 23.6 reduce-scatter.26
  629.0 20.0 reduce-scatter.28
  664.4 21.1 reduce-scatter.30
  702.5 23.5 reduce-scatter.32
  729.7 20.0 reduce-scatter.34
  753.5 130.6 reduce-scatter.38
  888.2 128.0 reduce-scatter.36
Sparse Core Ops, SparseCore 1:
  183.9 42.8 all-gather.20
  229.3 40.0 all-gather.22
  455.5 39.3 all-gather.24
  497.7 40.0 all-gather.26
where the time goes:
time: 1050 us; the launch traced here: 1040 us
  waiting for transfers between devices  440 us (42%)
  blocking collectives  409 us (39%)
  matrix products  72.4 us (7%)
  local copies, waits for them, and re-layouts  56.6 us (5%)
  other arithmetic  38.3 us (4%)
  between operations  17.5 us (2%)
    unnamed x18, waiting for transfers between devices  198 us
    all_gather x2, waiting for transfers between devices, per_device(): lax.all_gather(w_fc2[layer_params], ('seq', 'dp'), axis=0, tiled=True)  79.6 us
    all_gather x2, blocking collectives, per_device(): lax.all_gather(w_query[layer_params], ('seq', 'dp'), axis=0, tiled=True)  66.2 us
    all_gather x2, blocking collectives, per_device(): lax.all_gather(w_key[layer_params], ('seq', 'dp'), axis=0, tiled=True)  64.5 us
    all_gather x2, blocking collectives, per_device(): lax.all_gather(w_value[layer_params], ('seq', 'dp'), axis=0, tiled=True)  64.5 us
    all_gather x2, blocking collectives, per_device(): lax.all_gather(w_out[layer_params], ('seq', 'dp'), axis=0, tiled=True)  64.3 us
    reduce_scatter x4, waiting for transfers between devices, norm_total(): lax.psum_scatter(partial_value.astype(jnp.bfloat16), 'tensor', scatter_di...  54.5 us
    reduce_scatter x4, waiting for transfers between devices, branch_total(): lax.psum_scatter(partial_value.astype(jnp.bfloat16), 'tensor', scatter_di...  45.1 us
  transfers between devices with their start and end apart: 16, of which 14 were waited for; matrix products, arithmetic and copies ran while one was open for 8% of the time, Pallas kernels for 0%

commit v1 on v0

v1 whole, which is shorter than its diff:
```python
import functools
import math

import jax
import jax.numpy as jnp
from jax import lax
from jax.experimental import pallas as pl
from jax.experimental.pallas import tpu as pltpu
from jax.sharding import PartitionSpec as P

HEAD_DIM = 64


EPSILON = 1e-05
INV_ROOT_TWO = 1.0 / math.sqrt(2.0)
INV_ROOT_TWO_PI = 1.0 / math.sqrt(2.0 * math.pi)


def standardize_rows(values):
    center = values - jnp.mean(values, -1, keepdims=True)
    inverse_scale = lax.rsqrt(jnp.mean(center * center, -1, keepdims=True) + EPSILON)
    return (center * inverse_scale, inverse_scale)


def norm_backward_pass(output_gradient, centered_normalized, inverse_scale, norm_gain):
    scaled_values = output_gradient * norm_gain
    return inverse_scale * (
        scaled_values
        - jnp.mean(scaled_values, -1, keepdims=True)
        - centered_normalized * jnp.mean(scaled_values * centered_normalized, -1, keepdims=True)
    )


def times_trans(left, right):
    return lax.dot_general(
        left, right, (((1,), (1,)), ((), ())), preferred_element_type=jnp.float32
    )


def trans_times(left, right):
    return lax.dot_general(
        left, right, (((0,), (0,)), ((), ())), preferred_element_type=jnp.float32
    )


def matmul(left, right):
    return jnp.dot(left, right, preferred_element_type=jnp.float32)


def gelu_slope(pre_act):
    return (
        0.5 * (1.0 + jax.scipy.special.erf(pre_act * INV_ROOT_TWO))
        + pre_act * jnp.exp(-0.5 * pre_act * pre_act) * INV_ROOT_TWO_PI
    )


def split_heads(block):
    return block.reshape(block.shape[0], block.shape[1] // HEAD_DIM, HEAD_DIM)


def attend_forward(query_blk, key_blk, value_blk):
    scale = HEAD_DIM ** (-0.5)
    scores = (
        jnp.einsum(
            "qhd,khd->hqk",
            split_heads(query_blk),
            split_heads(key_blk),
            preferred_element_type=jnp.float32,
        )
        * scale
    )
    top = jnp.max(scores, -1, keepdims=True)
    expo = jnp.exp(scores - top)
    total = jnp.sum(expo, -1, keepdims=True)
    prob = (expo / total).astype(jnp.bfloat16)
    attended = jnp.einsum(
        "hqk,khd->qhd", prob, split_heads(value_blk), preferred_element_type=jnp.float32
    )
    attended = attended.reshape(query_blk.shape[0], -1).astype(jnp.bfloat16)
    return (attended, (top + jnp.log(total))[..., 0])


def score_grads(query_heads, key_heads, value_heads, log_total, grad_heads, inner):
    scale = HEAD_DIM ** (-0.5)
    scores = (
        jnp.einsum("qhd,khd->hqk", query_heads, key_heads, preferred_element_type=jnp.float32)
        * scale
    )
    prob = jnp.exp(scores - log_total[..., None])
    grad_prob = jnp.einsum(
        "qhd,khd->hqk", grad_heads, value_heads, preferred_element_type=jnp.float32
    )
    inner = jnp.sum(prob * grad_prob, -1)
    grad_scores = (prob * (grad_prob - inner[..., None])).astype(jnp.bfloat16)
    return (prob, grad_scores, inner)


def key_side(grad_scores, prob, query_heads, grad_heads, frames_all):
    scale = HEAD_DIM ** (-0.5)
    grad_key = (
        jnp.einsum("hqk,qhd->khd", grad_scores, query_heads, preferred_element_type=jnp.float32)
        * scale
    )
    grad_value = jnp.einsum(
        "hqk,qhd->khd", prob.astype(jnp.bfloat16), grad_heads, preferred_element_type=jnp.float32
    )
    return jnp.concatenate(
        [grad_key.reshape(frames_all, -1), grad_value.reshape(frames_all, -1)], 1
    )


def attend_backward(query_blk, key_blk, value_blk, log_total, grad_blk):
    query_heads = split_heads(query_blk)
    key_heads = split_heads(key_blk)
    grad_heads = split_heads(grad_blk)
    prob, grad_scores, inner = score_grads(
        query_heads, key_heads, split_heads(value_blk), log_total, grad_heads, None
    )
    grad_query = jnp.einsum(
        "hqk,khd->qhd", grad_scores, key_heads, preferred_element_type=jnp.float32
    ) * HEAD_DIM ** (-0.5)
    joined = key_side(grad_scores, prob, query_heads, grad_heads, key_blk.shape[0])
    return (grad_query.reshape(query_blk.shape[0], -1), joined)


MESH = pl.DeviceIdType.MESH
PIECES = 4


def tensor_sum_kernel(part_ref, out_ref, got_pair, mid, got_far, tot, got_back, *sems):
    send_a, recv_a, send_b, recv_b, send_c, recv_c = sems
    me = lax.axis_index("tensor")
    core = lax.rem(me, 2)
    pair = me + 1 - 2 * core
    far = lax.rem(me + 2, 4)
    barrier = pltpu.get_barrier_semaphore()
    for other in (pair, far):
        pl.semaphore_signal(barrier, inc=1, device_id={"tensor": other}, device_id_type=MESH)
    pl.semaphore_wait(barrier, 2)
    half = part_ref.shape[0] // 2
    step = half // PIECES
    mine = core * half
    theirs = (1 - core) * half

    def spot(base, piece):
        return pl.ds(pl.multiple_of(base + piece * step, step), step)

    def here(piece):
        return pl.ds(piece * step, step)

    firsts, seconds, thirds = [], [], []
    for piece in range(PIECES):
        copy = pltpu.make_async_remote_copy(
            src_ref=part_ref.at[spot(theirs, piece)],
            dst_ref=got_pair.at[here(piece)],
            send_sem=send_a.at[piece],
            recv_sem=recv_a.at[piece],
            device_id={"tensor": pair},
            device_id_type=MESH,
        )
        copy.start()
        firsts.append(copy)
    for piece in range(PIECES):
        firsts[piece].wait_recv()
        mid[here(piece)] = (
            part_ref[spot(mine, piece)].astype(jnp.float32)
            + got_pair[here(piece)].astype(jnp.float32)
        ).astype(jnp.bfloat16)
        copy = pltpu.make_async_remote_copy(
            src_ref=mid.at[here(piece)],
            dst_ref=got_far.at[here(piece)],
            send_sem=send_b.at[piece],
            recv_sem=recv_b.at[piece],
            device_id={"tensor": far},
            device_id_type=MESH,
        )
        copy.start()
        seconds.append(copy)
    for piece in range(PIECES):
        seconds[piece].wait_recv()
        total = mid[here(piece)].astype(jnp.float32) + got_far[here(piece)].astype(jnp.float32)
        tot[here(piece)] = total
        out_ref[spot(mine, piece)] = total
        copy = pltpu.make_async_remote_copy(
            src_ref=tot.at[here(piece)],
            dst_ref=got_back.at[here(piece)],
            send_sem=send_c.at[piece],
            recv_sem=recv_c.at[piece],
            device_id={"tensor": pair},
            device_id_type=MESH,
        )
        copy.start()
        thirds.append(copy)
    for piece in range(PIECES):
        thirds[piece].wait_recv()
        out_ref[spot(theirs, piece)] = got_back[here(piece)]
    for copy in firsts + seconds + thirds:
        copy.wait_send()


def tensor_sum(partial_value):
    rows, width = partial_value.shape
    half = rows // 2
    return pl.pallas_call(
        tensor_sum_kernel,
        out_shape=jax.ShapeDtypeStruct((rows, width), jnp.float32),
        in_specs=[pl.BlockSpec(memory_space=pltpu.VMEM)],
        out_specs=pl.BlockSpec(memory_space=pltpu.VMEM),
        scratch_shapes=[
            pltpu.VMEM((half, width), jnp.bfloat16),
            pltpu.VMEM((half, width), jnp.bfloat16),
            pltpu.VMEM((half, width), jnp.bfloat16),
            pltpu.VMEM((half, width), jnp.float32),
            pltpu.VMEM((half, width), jnp.float32),
        ]
        + [pltpu.SemaphoreType.DMA((PIECES,))] * 6,
        compiler_params=pltpu.CompilerParams(
            collective_id=0, has_side_effects=True, vmem_limit_bytes=16 * 2**20
        ),
        cost_estimate=pl.CostEstimate(
            flops=rows * width * 4, bytes_accessed=20_000_000, transcendentals=0
        ),
        name="tensor_sum",
    )(partial_value.astype(jnp.bfloat16))


def small_sum_kernel(count, dp_count, part_ref, out_ref, slots, own_sem, send_sem, recv_sem):
    me = lax.axis_index("seq") * dp_count + lax.axis_index("dp")

    def place(shift):
        other = lax.rem(me + shift, count)
        return {"seq": other // dp_count, "dp": lax.rem(other, dp_count)}

    barrier = pltpu.get_barrier_semaphore()
    for shift in range(1, count):
        pl.semaphore_signal(barrier, inc=1, device_id=place(shift), device_id_type=MESH)
    pl.semaphore_wait(barrier, count - 1)
    copies = []
    for shift in range(1, count):
        copy = pltpu.make_async_remote_copy(
            src_ref=part_ref,
            dst_ref=slots.at[me],
            send_sem=send_sem.at[shift],
            recv_sem=recv_sem.at[shift],
            device_id=place(shift),
            device_id_type=MESH,
        )
        copy.start()
        copies.append(copy)
    own = pltpu.make_async_copy(part_ref, slots.at[me], own_sem)
    own.start()
    own.wait()
    for copy in copies:
        copy.wait()
    total = slots[0]
    for index in range(1, count):
        total = total + slots[index]
    out_ref[...] = total


def small_sum(packed):
    count = lax.axis_size(("seq", "dp"))
    dp_count = lax.axis_size("dp")
    return pl.pallas_call(
        functools.partial(small_sum_kernel, count, dp_count),
        out_shape=jax.ShapeDtypeStruct(packed.shape, jnp.float32),
        in_specs=[pl.BlockSpec(memory_space=pltpu.VMEM)],
        out_specs=pl.BlockSpec(memory_space=pltpu.VMEM),
        scratch_shapes=[
            pltpu.VMEM((count,) + packed.shape, jnp.float32),
            pltpu.SemaphoreType.DMA,
            pltpu.SemaphoreType.DMA((count,)),
            pltpu.SemaphoreType.DMA((count,)),
        ],
        compiler_params=pltpu.CompilerParams(
            collective_id=1, has_side_effects=True, vmem_limit_bytes=16 * 2**20
        ),
        cost_estimate=pl.CostEstimate(flops=1000, bytes_accessed=20_000_000, transcendentals=0),
        name="small_sum",
    )(packed)


def per_device(
    inputs,
    cotangent,
    attention_norm_gain,
    attention_norm_bias,
    w_query,
    b_query,
    w_key,
    w_value,
    b_value,
    w_out,
    b_out,
    feedforward_norm_gain,
    feedforward_norm_bias,
    w_fc1,
    b_fc1,
    w_fc2,
    b_fc2,
):
    clips, frames_local, width = inputs.shape
    rows = clips * frames_local
    layers = w_query.shape[0]
    cols = w_query.shape[2]
    hidden = w_fc1.shape[2]
    group = ("seq", "dp")
    hidden_state = inputs.astype(jnp.float32).reshape(rows, width)
    full_first, full_rest = [], []
    for layer in range(layers):
        first = jnp.concatenate([w_query[layer], w_key[layer], w_value[layer]], 1)
        rest = jnp.concatenate([w_fc1[layer], w_fc2[layer], w_out[layer]], 1)
        full_first.append(lax.all_gather(first, group, axis=0, tiled=True))
        full_rest.append(lax.all_gather(rest, group, axis=0, tiled=True))
    saved_all = []
    for layer in range(layers):
        full_qkv = full_first[layer]
        full_up = full_rest[layer][:, :hidden]
        full_down = full_rest[layer][:, hidden : 2 * hidden]
        full_o = full_rest[layer][:, 2 * hidden :]
        xhat1, rstd1 = standardize_rows(hidden_state)
        normed1 = (xhat1 * attention_norm_gain[layer] + attention_norm_bias[layer]).astype(
            jnp.bfloat16
        )
        bias = jnp.concatenate([b_query[layer], jnp.zeros_like(b_query[layer]), b_value[layer]])
        qkv = (matmul(normed1, full_qkv) + bias).astype(jnp.bfloat16)
        queries = qkv[:, :cols].reshape(clips, frames_local, cols)
        kv_local = qkv[:, cols:].reshape(clips, frames_local, 2 * cols)
        kv_all = lax.all_gather(kv_local, "seq", axis=1, tiled=True)
        outcomes = [
            attend_forward(queries[clip], kv_all[clip, :, :cols], kv_all[clip, :, cols:])
            for clip in range(clips)
        ]
        log_total = [outcome[1] for outcome in outcomes]
        attended = jnp.concatenate([outcome[0] for outcome in outcomes], 0)
        middle_state = hidden_state + (tensor_sum(times_trans(attended, full_o)) + b_out[layer])
        xhat2, rstd2 = standardize_rows(middle_state)
        normed2 = (xhat2 * feedforward_norm_gain[layer] + feedforward_norm_bias[layer]).astype(
            jnp.bfloat16
        )
        pre_act = matmul(normed2, full_up) + b_fc1[layer]
        activated = jax.nn.gelu(pre_act, approximate=False).astype(jnp.bfloat16)
        hidden_state = middle_state + (
            tensor_sum(times_trans(activated, full_down)) + b_fc2[layer]
        )
        saved_all.append(
            (xhat1, rstd1, normed1, queries, kv_all, log_total, attended, xhat2, rstd2, normed2, pre_act, activated)
        )
    encoded = hidden_state.reshape(clips, frames_local, width)
    state_gradient = cotangent.reshape(rows, width)
    grads_first, grads_rest, smalls = [None] * layers, [None] * layers, [None] * layers
    for layer in reversed(range(layers)):
        full_qkv = full_first[layer]
        full_up = full_rest[layer][:, :hidden]
        full_down = full_rest[layer][:, hidden : 2 * hidden]
        full_o = full_rest[layer][:, 2 * hidden :]
        (xhat1, rstd1, normed1, queries, kv_all, log_total, attended, xhat2, rstd2, normed2, pre_act, activated) = saved_all[layer]
        grad_mlp = state_gradient.astype(jnp.bfloat16)
        grad_pre = (matmul(grad_mlp, full_down) * gelu_slope(pre_act)).astype(jnp.bfloat16)
        grad_norm2 = tensor_sum(times_trans(grad_pre, full_up))
        middle_gradient = state_gradient + norm_backward_pass(
            grad_norm2, xhat2, rstd2, feedforward_norm_gain[layer]
        )
        grad_attn = middle_gradient.astype(jnp.bfloat16)
        rest_terms = jnp.concatenate(
            [
                trans_times(normed2, grad_pre).astype(jnp.bfloat16),
                trans_times(grad_mlp, activated).astype(jnp.bfloat16),
                trans_times(grad_attn, attended).astype(jnp.bfloat16),
            ],
            1,
        )
        grads_rest[layer] = lax.psum_scatter(rest_terms, group, scatter_dimension=0, tiled=True)
        grad_attended = (
            matmul(grad_attn, full_o).astype(jnp.bfloat16).reshape(clips, frames_local, cols)
        )
        outcomes = [
            attend_backward(
                queries[clip],
                kv_all[clip, :, :cols],
                kv_all[clip, :, cols:],
                log_total[clip],
                grad_attended[clip],
            )
            for clip in range(clips)
        ]
        kv_terms = jnp.stack([outcome[1] for outcome in outcomes], 0).astype(jnp.bfloat16)
        kv_grads = lax.psum_scatter(kv_terms, "seq", scatter_dimension=1, tiled=True)
        grad_query = jnp.concatenate([outcome[0] for outcome in outcomes], 0).astype(jnp.bfloat16)
        grad_qkv = jnp.concatenate([grad_query, kv_grads.reshape(rows, 2 * cols)], 1)
        grads_first[layer] = lax.psum_scatter(
            trans_times(normed1, grad_qkv).astype(jnp.bfloat16),
            group,
            scatter_dimension=0,
            tiled=True,
        )
        grad_norm1 = tensor_sum(times_trans(grad_qkv, full_qkv))
        state_gradient = middle_gradient + norm_backward_pass(
            grad_norm1, xhat1, rstd1, attention_norm_gain[layer]
        )
        sums_qkv = jnp.sum(grad_qkv, 0, dtype=jnp.float32)
        smalls[layer] = (
            jnp.sum(grad_norm1 * xhat1, 0),
            jnp.sum(grad_norm1, 0),
            sums_qkv[:cols],
            sums_qkv[2 * cols :],
            jnp.sum(grad_attn, 0, dtype=jnp.float32),
            jnp.sum(grad_norm2 * xhat2, 0),
            jnp.sum(grad_norm2, 0),
            jnp.sum(grad_pre, 0, dtype=jnp.float32),
            jnp.sum(grad_mlp, 0, dtype=jnp.float32),
        )
    flat = jnp.concatenate([part for layer in range(layers) for part in smalls[layer]])
    length = flat.shape[0]
    padded = -(-length // 1024) * 1024
    packed = jnp.pad(flat, (0, padded - length)).reshape(padded // 128, 128)
    summed = small_sum(packed).reshape(padded)
    small_stack, offset = [[] for _ in range(9)], 0
    for layer in range(layers):
        for member in range(9):
            size = smalls[layer][member].shape[0]
            small_stack[member].append(summed[offset : offset + size])
            offset += size
    small_stack = [jnp.stack(members, 0) for members in small_stack]
    first_out = [grad.astype(jnp.float32) for grad in grads_first]
    rest_out = [grad.astype(jnp.float32) for grad in grads_rest]

    def pick(parts, start, size):
        return jnp.stack([part[:, start : start + size] for part in parts], 0)

    grad_inputs = state_gradient.reshape(clips, frames_local, width)
    return (
        encoded,
        grad_inputs,
        small_stack[0],
        small_stack[1],
        pick(first_out, 0, cols),
        small_stack[2],
        pick(first_out, cols, cols),
        pick(first_out, 2 * cols, cols),
        small_stack[3],
        pick(rest_out, 2 * hidden, cols),
        small_stack[4],
        small_stack[5],
        small_stack[6],
        pick(rest_out, 0, hidden),
        small_stack[7],
        pick(rest_out, hidden, hidden),
        small_stack[8],
    )


def solution(mesh):
    placed = (
        P("dp", "seq", None),
        P("dp", "seq", None),
        P(),
        P(),
        P(None, ("seq", "dp"), "tensor"),
        P(None, "tensor"),
        P(None, ("seq", "dp"), "tensor"),
        P(None, ("seq", "dp"), "tensor"),
        P(None, "tensor"),
        P(None, ("seq", "dp"), "tensor"),
        P(),
        P(),
        P(),
        P(None, ("seq", "dp"), "tensor"),
        P(None, "tensor"),
        P(None, ("seq", "dp"), "tensor"),
        P(),
    )
    return jax.shard_map(
        per_device,
        mesh=mesh,
        in_specs=placed,
        out_specs=(
            P("dp", "seq", None),
            P("dp", "seq", None),
            P(),
            P(),
            P(None, ("seq", "dp"), "tensor"),
            P(None, "tensor"),
            P(None, ("seq", "dp"), "tensor"),
            P(None, ("seq", "dp"), "tensor"),
            P(None, "tensor"),
            P(None, ("seq", "dp"), "tensor"),
            P(),
            P(),
            P(),
            P(None, ("seq", "dp"), "tensor"),
            P(None, "tensor"),
            P(None, ("seq", "dp"), "tensor"),
            P(),
        ),
        check_vma=False,
    )
```

time: 1050 us -> 594 us (0.57)
  blocking collectives: 409 us -> 120 us
  waiting for transfers between devices: 440 us -> 266 us
  Pallas kernels: 0 us -> 86.7 us
  matrix products: 72.4 us -> 39 us
  local copies, waits for them, and re-layouts: 56.6 us -> 28.3 us
    all_gather x20 -> x4, blocking collectives: 370 us -> 120 us  [the longest x2 74.2 us: per_device(): full_first.append(lax.all_gather(first, group, axis=0, tiled=True))]
    all_gather x4 -> x2, waiting for transfers between devices: 110 us -> 0.01 us  [per_device(): full_rest.append(lax.all_gather(rest, group, axis=0, tiled=True))]
    pallas_call x0 -> x9, Pallas kernels: none -> 86.7 us  [the longest x8 75.7 us: tensor_sum(): pl.pallas_call(tensor_sum_kernel, out_shape=jax.ShapeDtypeStruct((rows, w...]
    unnamed x18 -> x10, waiting for transfers between devices: 198 us -> 143 us
    psum x1 -> x0, blocking collectives: 38.7 us -> none  [per_device(): lax.psum((jnp.sum(first_norm_gradient * first_centered_normalized, 0), jn...]
    unnamed x220 -> x256, local copies, waits for them, and re-layouts: 38.4 us -> 22.3 us
    dot_general x12 -> x8, matrix products: 22.9 us -> 7.53 us  [times_trans(): lax.dot_general(left, right, (((1,), (1,)), ((), ())), preferred_element_...]
    dot_general x12 -> x8, matrix products: 24 us -> 9 us  [trans_times(): lax.dot_general(left, right, (((0,), (0,)), ((), ())), preferred_element_...]
  transfers between devices with their start and end apart: 16 -> 8, of which waited for: 14 -> 6; matrix products, arithmetic and copies ran while one was open for 8% -> 9% of each run, Pallas kernels for 0% -> 7%
where the time goes in v1:
time: 594 us; the launch traced here: 587 us
  waiting for transfers between devices  266 us (45%)
  blocking collectives  120 us (20%)
  Pallas kernels  86.7 us (15%)
  matrix products  39 us (7%)
  other arithmetic  29.7 us (5%)
  local copies, waits for them, and re-layouts  28.3 us (5%)
  between operations  16.4 us (3%)
    unnamed x10, waiting for transfers between devices  143 us
    reduce_scatter x2, waiting for transfers between devices, per_device(): lax.psum_scatter(trans_times(normed1, grad_qkv).astype(jnp.bfloat16), gro...  84.4 us
    pallas_call x8, Pallas kernels, tensor_sum(): pl.pallas_call(tensor_sum_kernel, out_shape=jax.ShapeDtypeStruct((rows, w...  75.7 us
    all_gather x2, blocking collectives, per_device(): full_first.append(lax.all_gather(first, group, axis=0, tiled=True))  74.2 us
    all_gather x2, blocking collectives, per_device(): kv_all = lax.all_gather(kv_local, 'seq', axis=1, tiled=True)  45.7 us
    reduce_scatter x2, waiting for transfers between devices, per_device(): lax.psum_scatter(kv_terms, 'seq', scatter_dimension=1, tiled=True)  39.3 us
    unnamed x256, local copies, waits for them, and re-layouts  22.3 us
  transfers between devices with their start and end apart: 8, of which 6 were waited for; matrix products, arithmetic and copies ran while one was open for 9% of the time, Pallas kernels for 7%

profile of v1, /device:TPU:0, one launch (start us, length us, event | category | flops | bytes accessed | tf_op | source)
XLA Modules:
  0.0 587.1 jit_solution(7210793437314115718)
XLA Ops:
  11.8 36.4 %all_gather.18 = bf16[768,576]{1,0:T(8,128)(2,1)S(1)} all-gather(bf16[96,576]{1,0:T(8,128)(2,1)S(1)} %pad_maximum_fusion.14), channel_id=1, replica_groups=mesh['tensor'=4,'seq'=4,'dp'=2] {'seq','dp'}, dimensions={0}, use_global_device_ids=true | all-gather | bytes 995328 | tf_op jit(solution)/shard_map/all_gather | solution.py:313
  50.9 27.7 %all-gather = bf16[1024,384]{0,1:T(8,128)(2,1)S(1)} all-gather(bf16[256,384]{0,1:T(8,128)(2,1)S(1)} %slice.340), channel_id=2, replica_groups=mesh['tensor'=4,'seq'=4,'dp'=2] {'seq'}, dimensions={0}, use_global_device_ids=true | all-gather | bytes 983040 | tf_op jit(solution)/shard_map/all_gather | solution.py:329
  78.8 37.8 %all_gather.21 = bf16[768,576]{1,0:T(8,128)(2,1)} all-gather(bf16[96,576]{1,0:T(8,128)(2,1)S(1)} %pad_maximum_fusion.15), channel_id=1, replica_groups=mesh['tensor'=4,'seq'=4,'dp'=2] {'seq','dp'}, dimensions={0}, use_global_device_ids=true | all-gather | bytes 995328 | tf_op jit(solution)/shard_map/all_gather | solution.py:313
  122.8 9.6 %tensor_sum.8 = f32[256,768]{1,0:T(8,128)S(1)} custom-call(bf16[256,768]{1,0:T(8,128)(2,1)S(1)} %convolution_convert_fusion.13.part_ref), custom_call_target="tpu_custom_call" | custom-call | flops 786432 | bytes 20000000 | tf_op jit(solution)/shard_map/tensor_sum/pallas_call | solution.py:204
  133.6 2.9 fusion.59
  137.9 9.6 %tensor_sum.9 = f32[256,768]{1,0:T(8,128)S(1)} custom-call(bf16[256,768]{1,0:T(8,128)(2,1)S(1)} %convolution_convert_fusion.12.part_ref), custom_call_target="tpu_custom_call" | custom-call | flops 786432 | bytes 20000000 | tf_op jit(solution)/shard_map/tensor_sum/pallas_call | solution.py:204
  148.6 18.0 %all-gather.1 = bf16[1024,384]{0,1:T(8,128)(2,1)S(1)} all-gather(bf16[256,384]{0,1:T(8,128)(2,1)S(1)} %slice.347), channel_id=3, replica_groups=mesh['tensor'=4,'seq'=4,'dp'=2] {'seq'}, dimensions={0}, use_global_device_ids=true | all-gather | bytes 983040 | tf_op jit(solution)/shard_map/all_gather | solution.py:329
  174.0 8.7 %tensor_sum.10 = f32[256,768]{1,0:T(8,128)S(1)} custom-call(bf16[256,768]{1,0:T(8,128)(2,1)S(1)} %convolution_convert_fusion.11.part_ref), custom_call_target="tpu_custom_call" | custom-call | flops 786432 | bytes 20000000 | tf_op jit(solution)/shard_map/tensor_sum/pallas_call | solution.py:204
  188.1 9.6 %tensor_sum.12 = f32[256,768]{1,0:T(8,128)S(1)} custom-call(bf16[256,768]{1,0:T(8,128)(2,1)S(1)} %convolution_convert_fusion.9.part_ref), custom_call_target="tpu_custom_call" | custom-call | flops 786432 | bytes 20000000 | tf_op jit(solution)/shard_map/tensor_sum/pallas_call | solution.py:204
  199.2 9.6 %tensor_sum.11 = f32[256,768]{1,0:T(8,128)S(1)} custom-call(bf16[256,768]{1,0:T(8,128)(2,1)S(1)} %convolution_convert_fusion.10.part_ref), custom_call_target="tpu_custom_call" | custom-call | flops 786432 | bytes 20000000 | tf_op jit(solution)/shard_map/tensor_sum/pallas_call | solution.py:204
  217.3 2.8 fusion.28
  220.0 20.9 %reduce-scatter.11.cloned.1.call-done = bf16[1,256,384]{1,2,0:T(8,128)(2,1)} async-done(((bf16[1,1024,384]{1,2,0:T(8,128)(2,1)}), bf16[1,256,384]{1,2,0:T(8,128)(2,1)}) %reduce-scatter.11.cloned.1.call-update) | async-done | bytes 196624 | tf_op jit(solution)/shard_map/reduce_scatter | solution.py:388
  242.9 9.6 %tensor_sum.13 = f32[256,768]{1,0:T(8,128)S(1)} custom-call(bf16[256,768]{1,0:T(8,128)(2,1)S(1)} %convolution_convert_fusion.8.part_ref), custom_call_target="tpu_custom_call" | custom-call | flops 786432 | bytes 20000000 | tf_op jit(solution)/shard_map/tensor_sum/pallas_call | solution.py:204
  256.8 9.6 %tensor_sum.14 = f32[256,768]{1,0:T(8,128)S(1)} custom-call(bf16[256,768]{1,0:T(8,128)(2,1)S(1)} %convolution_convert_fusion.7.part_ref), custom_call_target="tpu_custom_call" | custom-call | flops 786432 | bytes 20000000 | tf_op jit(solution)/shard_map/tensor_sum/pallas_call | solution.py:204
  274.4 2.7 convolution_convert_fusion.4
  277.8 18.4 %reduce-scatter.13.cloned.1.call-done = bf16[1,256,384]{1,2,0:T(8,128)(2,1)} async-done(((bf16[1,1024,384]{1,2,0:T(8,128)(2,1)}), bf16[1,256,384]{1,2,0:T(8,128)(2,1)}) %reduce-scatter.13.cloned.1.call-update) | async-done | bytes 196624 | tf_op jit(solution)/shard_map/reduce_scatter | solution.py:388
  301.6 4.3 copy.42
  308.5 4.3 copy.40
  314.7 9.6 %tensor_sum.15 = f32[256,768]{1,0:T(8,128)S(1)} custom-call(bf16[256,768]{1,0:T(8,128)(2,1)S(1)} %convolution_convert_fusion.6.part_ref), custom_call_target="tpu_custom_call" | custom-call | flops 786432 | bytes 20000000 | tf_op jit(solution)/shard_map/tensor_sum/pallas_call | solution.py:204
  325.1 10.9 %small_sum.1 = f32[96,128]{1,0:T(8,128)S(1)} custom-call(f32[96,128]{1,0:T(8,128)S(1)} %pad_bitcast_fusion.part_ref), custom_call_target="tpu_custom_call" | custom-call | flops 1000 | bytes 20000000 | tf_op jit(solution)/shard_map/small_sum/pallas_call | solution.py:264
  342.9 19.5 %reduce-scatter.17.cloned.1.call-done = bf16[96,576]{1,0:T(8,128)(2,1)} async-done(((bf16[768,576]{1,0:T(8,128)(2,1)}), bf16[96,576]{1,0:T(8,128)(2,1)}) %reduce-scatter.17.cloned.1.call-update) | async-done | bytes 110608 | tf_op jit(solution)/shard_map/reduce_scatter | solution.py:391
  363.5 64.8 %reduce-scatter.15.cloned.1.call-done = bf16[96,576]{1,0:T(8,128)(2,1)} async-done(((bf16[768,576]{1,0:T(8,128)(2,1)}), bf16[96,576]{1,0:T(8,128)(2,1)}) %reduce-scatter.15.cloned.1.call-update) | async-done | bytes 110608 | tf_op jit(solution)/shard_map/reduce_scatter | solution.py:391
  431.4 70.7 %reduce-scatter.21.cloned.1.call-done = bf16[96,1728]{1,0:T(8,128)(2,1)} async-done(((bf16[768,1728]{1,0:T(8,128)(2,1)}), bf16[96,1728]{1,0:T(8,128)(2,1)}) %reduce-scatter.21.cloned.1.call-update) | async-done | bytes 331792
  503.5 71.9 %reduce-scatter.19.cloned.1.call-done = bf16[96,1728]{1,0:T(8,128)(2,1)} async-done(((bf16[768,1728]{1,0:T(8,128)(2,1)}), bf16[96,1728]{1,0:T(8,128)(2,1)}) %reduce-scatter.19.cloned.1.call-update) | async-done | bytes 331792
  (401 shorter events, 81.1 us)
Async XLA Ops:
  7.3 114.0 %all-gather.5.cloned.1.call-start = ((), (), s32[]{:S(2)}) async-start(), calls=%async_computation.6 | async-start | bytes 3096576 | tf_op jit(solution)/shard_map/all_gather | solution.py:314
  8.2 39.9 %copy-start.100 = (f32[2,768]{1,0:T(2,128)S(1)}, f32[2,768]{1,0:T(2,128)}, u32[]{:S(2)}) copy-start(f32[2,768]{1,0:T(2,128)} %param.20) | copy-start | bytes 18436
  8.2 39.9 %copy-start.101 = (f32[2,768]{1,0:T(2,128)S(1)}, f32[2,768]{1,0:T(2,128)}, u32[]{:S(2)}) copy-start(f32[2,768]{1,0:T(2,128)} %param.19) | copy-start | bytes 18436
  10.2 162.2 %all-gather.7.cloned.1.call-start = ((), (), s32[]{:S(2)}) async-start(), calls=%async_computation.7 | async-start | bytes 3096576 | tf_op jit(solution)/shard_map/all_gather | solution.py:314
  11.0 229.9 %reduce-scatter.11.cloned.1.call-start = ((), (), s32[]{:S(2)}) async-start(), calls=%async_computation.8 | async-start | bytes 983040 | tf_op jit(solution)/shard_map/reduce_scatter | solution.py:388
  11.2 39.0 %copy-start.102 = (f32[2,768]{1,0:T(2,128)S(1)}, f32[2,768]{1,0:T(2,128)}, u32[]{:S(2)}) copy-start(f32[2,768]{1,0:T(2,128)} %param.27) | copy-start | bytes 18436
  11.3 67.3 %copy-start.75 = (f32[256]{0:T(256)}, f32[256]{0:T(256)S(1)}, u32[]{:S(2)}) copy-start(f32[256]{0:T(256)S(1)} %broadcast_multiply_fusion.11) | copy-start | bytes 3076
  11.5 67.0 %copy-start.96 = (f32[256]{0:T(256)}, f32[256]{0:T(256)S(1)}, u32[]{:S(2)}) copy-start(f32[256]{0:T(256)S(1)} %add_rsqrt_fusion.3) | copy-start | bytes 3076
  48.2 30.5 %copy-start.30 = (bf16[768,576]{1,0:T(8,128)(2,1)}, bf16[768,576]{1,0:T(8,128)(2,1)S(1)}, u32[]{:S(2)}) copy-start(bf16[768,576]{1,0:T(8,128)(2,1)S(1)} %all_gather.18) | copy-start | bytes 2654212
  48.8 29.8 %copy-start.57 = (f32[768]{0:T(1024)}, f32[768]{0:T(1024)S(1)}, u32[]{:S(2)}) copy-start(f32[768]{0:T(1024)S(1)} %get-tuple-element.169) | copy-start | bytes 9220
  48.8 29.8 %copy-start.109 = (f32[768]{0:T(1024)}, f32[768]{0:T(1024)S(1)}, u32[]{:S(2)}) copy-start(f32[768]{0:T(1024)S(1)} %get-tuple-element.80) | copy-start | bytes 9220
  50.2 66.4 %copy-start.103 = (f32[2,768]{1,0:T(2,128)S(1)}, f32[2,768]{1,0:T(2,128)}, u32[]{:S(2)}) copy-start(f32[2,768]{1,0:T(2,128)} %param.33) | copy-start | bytes 18436
  50.2 66.4 %copy-start.104 = (f32[2,768]{1,0:T(2,128)S(1)}, f32[2,768]{1,0:T(2,128)}, u32[]{:S(2)}) copy-start(f32[2,768]{1,0:T(2,128)} %param.28) | copy-start | bytes 18436
  50.2 67.0 %copy-start.105 = (f32[2,768]{1,0:T(2,128)S(1)}, f32[2,768]{1,0:T(2,128)}, u32[]{:S(2)}) copy-start(f32[2,768]{1,0:T(2,128)} %param.31) | copy-start | bytes 18436
  50.2 67.0 %copy-start.106 = (f32[2,768]{1,0:T(2,128)S(1)}, f32[2,768]{1,0:T(2,128)}, u32[]{:S(2)}) copy-start(f32[2,768]{1,0:T(2,128)} %param.29) | copy-start | bytes 18436
  50.2 68.3 %copy-start.34 = (bf16[256,192]{0,1:T(8,128)(2,1)}, bf16[256,192]{0,1:T(8,128)(2,1)S(1)}, u32[]{:S(2)}) copy-start(bf16[256,192]{0,1:T(8,128)(2,1)S(1)} %slice.342) | copy-start | bytes 294916
  78.7 39.1 %copy-start.22 = (bf16[1,1024,192]{1,2,0:T(8,128)(2,1)}, bf16[1,1024,192]{1,2,0:T(8,128)(2,1)S(1)}, u32[]{:S(2)}) copy-start(bf16[1,1024,192]{1,2,0:T(8,128)(2,1)S(1)} %get-tuple-element.101) | copy-start | bytes 1179652
  78.7 40.5 %copy-start.26 = (bf16[1,1024,192]{1,2,0:T(8,128)(2,1)}, bf16[1,1024,192]{1,2,0:T(8,128)(2,1)S(1)}, u32[]{:S(2)}) copy-start(bf16[1,1024,192]{1,2,0:T(8,128)(2,1)S(1)} %get-tuple-element.102) | copy-start | bytes 1179652
  216.3 79.9 %reduce-scatter.13.cloned.1.call-start = ((), (), s32[]{:S(2)}) async-start(), calls=%async_computation.9 | async-start | bytes 983040 | tf_op jit(solution)/shard_map/reduce_scatter | solution.py:388
  274.4 88.1 %reduce-scatter.17.cloned.1.call-start = ((), (), s32[]{:S(2)}) async-start(), calls=%async_computation.11 | async-start | bytes 1105920 | tf_op jit(solution)/shard_map/reduce_scatter | solution.py:391
  277.1 151.2 %reduce-scatter.15.cloned.1.call-start = ((), (), s32[]{:S(2)}) async-start(), calls=%async_computation.10 | async-start | bytes 1105920 | tf_op jit(solution)/shard_map/reduce_scatter | solution.py:391
  298.9 203.2 %reduce-scatter.21.cloned.1.call-start = ((), (), s32[]{:S(2)}) async-start(), calls=%async_computation.13 | async-start | bytes 3096576
  306.0 269.4 %reduce-scatter.19.cloned.1.call-start = ((), (), s32[]{:S(2)}) async-start(), calls=%async_computation.12 | async-start | bytes 3096576
  314.0 27.7 %copy-start.78 = (f32[256]{0:T(256)S(1)}, f32[256]{0:T(256)}, u32[]{:S(2)}) copy-start(f32[256]{0:T(256)} %copy-done.75) | copy-start | bytes 3076
  (101 other events, 908.3 us)
Sparse Core Ops, SparseCore 0:
  10.8 75.5 all-gather.4
  89.2 58.8 all-gather.6
  216.4 24.4 reduce-scatter.10
  274.4 21.7 reduce-scatter.12
  299.4 62.9 reduce-scatter.16
  366.0 62.2 reduce-scatter.14
  431.8 70.1 reduce-scatter.20
  505.6 69.7 reduce-scatter.18

commit v2 on v1

--- a/solution.py
+++ b/solution.py
@@ -224,60 +224,247 @@
     )(partial_value.astype(jnp.bfloat16))
 
 
-def small_sum_kernel(count, dp_count, part_ref, out_ref, slots, own_sem, send_sem, recv_sem):
-    me = lax.axis_index("seq") * dp_count + lax.axis_index("dp")
+def gather_kernel(seqs, dps, forward, own_ref, out_ref, own_sem, send_z, recv_z, *sems):
+    s, d = lax.axis_index("seq"), lax.axis_index("dp")
+
+    def along(k):
+        return {"seq": lax.rem(s + k, seqs)}
+
+    def across(j):
+        return {"dp": lax.rem(d + j, dps)}
+
+    def slot(k):
+        source = lax.rem(s + seqs - k, seqs)
+        return source * dps + d if forward else source
+
+    barrier = pltpu.get_barrier_semaphore()
+    others = [along(k) for k in range(1, seqs)]
+    if forward:
+        others += [across(j) for j in range(1, dps)]
+    for other in others:
+        pl.semaphore_signal(barrier, inc=1, device_id=other, device_id_type=MESH)
+    pl.semaphore_wait(barrier, len(others))
+    firsts, seconds = [], []
+    for k in range(1, seqs):
+        copy = pltpu.make_async_remote_copy(
+            src_ref=own_ref,
+            dst_ref=out_ref.at[slot(0)],
+            send_sem=send_z.at[k],
+            recv_sem=recv_z.at[k],
+            device_id=along(k),
+            device_id_type=MESH,
+        )
+        copy.start()
+        firsts.append(copy)
+    own = pltpu.make_async_copy(own_ref, out_ref.at[slot(0)], own_sem)
+    own.start()
+    for k in (0, 1, seqs - 1) + tuple(range(2, seqs - 1)):
+        if k:
+            firsts[k - 1].wait_recv()
+        if forward:
+            send_y, recv_y = sems
+            for j in range(1, dps):
+                copy = pltpu.make_async_remote_copy(
+                    src_ref=out_ref.at[slot(k)] if k else own_ref,
+                    dst_ref=out_ref.at[slot(k)],
+                    send_sem=send_y.at[k * dps + j],
+                    recv_sem=recv_y.at[k * dps + j],
+                    device_id=across(j),
+                    device_id_type=MESH,
+                )
+                copy.start()
+                seconds.append(copy)
+    own.wait()
+    for copy in firsts:
+        copy.wait_send()
+    for copy in seconds:
+        copy.wait()
+
+
+def gather_slots(block, forward):
+    seqs, dps = lax.axis_size("seq"), lax.axis_size("dp")
+    count = seqs * dps if forward else seqs
+    sems = [pltpu.SemaphoreType.DMA((seqs,))] * 2
+    if forward:
+        sems += [pltpu.SemaphoreType.DMA((seqs * dps,))] * 2
+    return pl.pallas_call(
+        functools.partial(gather_kernel, seqs, dps, forward),
+        out_shape=jax.ShapeDtypeStruct((count,) + block.shape, block.dtype),
+        in_specs=[pl.BlockSpec(memory_space=pl.ANY)],
+        out_specs=pl.BlockSpec(memory_space=pl.ANY),
+        scratch_shapes=[pltpu.SemaphoreType.DMA] + sems,
+        compiler_params=pltpu.CompilerParams(
+            collective_id=2 if forward else 3, has_side_effects=True, vmem_limit_bytes=16 * 2**20
+        ),
+        cost_estimate=pl.CostEstimate(
+            flops=1000, bytes_accessed=100_000_000 if forward else 40_000_000, transcendentals=0
+        ),
+        name="gather_weights" if forward else "gather_frames",
+    )(block)
+
+
+def frame_sum_kernel(seqs, part_ref, out_ref, got, send_sem, recv_sem):
+    s = lax.axis_index("seq")
+    barrier = pltpu.get_barrier_semaphore()
+    for k in range(1, seqs):
+        pl.semaphore_signal(
+            barrier, inc=1, device_id={"seq": lax.rem(s + k, seqs)}, device_id_type=MESH
+        )
+    pl.semaphore_wait(barrier, seqs - 1)
+    copies = []
+    for k in range(1, seqs):
+        other = lax.rem(s + k, seqs)
+        copy = pltpu.make_async_remote_copy(
+            src_ref=part_ref.at[other],
+            dst_ref=got.at[k],
+            send_sem=send_sem.at[k],
+            recv_sem=recv_sem.at[k],
+            device_id={"seq": other},
+            device_id_type=MESH,
+        )
+        copy.start()
+        copies.append(copy)
+    for copy in copies:
+        copy.wait_recv()
+    total = part_ref[s].astype(jnp.float32)
+    for k in range(1, seqs):
+        total = total + got[k].astype(jnp.float32)
+    out_ref[...] = total.astype(jnp.bfloat16)
+    for copy in copies:
+        copy.wait_send()
+
+
+def frame_sum(parts):
+    seqs = lax.axis_size("seq")
+    return pl.pallas_call(
+        functools.partial(frame_sum_kernel, seqs),
+        out_shape=jax.ShapeDtypeStruct(parts.shape[1:], jnp.bfloat16),
+        in_specs=[pl.BlockSpec(memory_space=pltpu.VMEM)],
+        out_specs=pl.BlockSpec(memory_space=pltpu.VMEM),
+        scratch_shapes=[
+            pltpu.VMEM(parts.shape, jnp.bfloat16),
+            pltpu.SemaphoreType.DMA((seqs,)),
+            pltpu.SemaphoreType.DMA((seqs,)),
+        ],
+        compiler_params=pltpu.CompilerParams(
+            collective_id=4, has_side_effects=True, vmem_limit_bytes=16 * 2**20
+        ),
+        cost_estimate=pl.CostEstimate(flops=1000, bytes_accessed=40_000_000, transcendentals=0),
+        name="frame_sum",
+    )(parts)
+
+
+def grad_sum_kernel(
+    seqs, dps, part_ref, small_ref, out_ref, small_out, got_y, mid, got_z, slots,
+    own_sem, send_s, recv_s, send_y, recv_y, send_z, recv_z,
+):
+    s, d = lax.axis_index("seq"), lax.axis_index("dp")
+    count = seqs * dps
+    me = s * dps + d
 
     def place(shift):
         other = lax.rem(me + shift, count)
-        return {"seq": other // dp_count, "dp": lax.rem(other, dp_count)}
+        return {"seq": other // dps, "dp": lax.rem(other, dps)}
 
     barrier = pltpu.get_barrier_semaphore()
     for shift in range(1, count):
         pl.semaphore_signal(barrier, inc=1, device_id=place(shift), device_id_type=MESH)
     pl.semaphore_wait(barrier, count - 1)
-    copies = []
+    order = tuple(range(1, seqs)) + (0,)
+    firsts, seconds, smalls = {}, {}, []
+    for k in order:
+        for j in range(1, dps):
+            to = lax.rem(d + j, dps)
+            copy = pltpu.make_async_remote_copy(
+                src_ref=part_ref.at[lax.rem(s + k, seqs) * dps + to],
+                dst_ref=got_y.at[k * dps + j],
+                send_sem=send_y.at[k * dps + j],
+                recv_sem=recv_y.at[k * dps + j],
+                device_id={"dp": to},
+                device_id_type=MESH,
+            )
+            copy.start()
+            firsts[k, j] = copy
     for shift in range(1, count):
         copy = pltpu.make_async_remote_copy(
-            src_ref=part_ref,
+            src_ref=small_ref,
             dst_ref=slots.at[me],
-            send_sem=send_sem.at[shift],
-            recv_sem=recv_sem.at[shift],
+            send_sem=send_s.at[shift],
+            recv_sem=recv_s.at[shift],
             device_id=place(shift),
             device_id_type=MESH,
         )
         copy.start()
-        copies.append(copy)
-    own = pltpu.make_async_copy(part_ref, slots.at[me], own_sem)
+        smalls.append(copy)
+    own = pltpu.make_async_copy(small_ref, slots.at[me], own_sem)
     own.start()
+    for k in order:
+        total = part_ref[lax.rem(s + k, seqs) * dps + d].astype(jnp.float32)
+        for j in range(1, dps):
+            firsts[k, j].wait_recv()
+            total = total + got_y[k * dps + j].astype(jnp.float32)
+        if k:
+            mid[k] = total.astype(jnp.bfloat16)
+            copy = pltpu.make_async_remote_copy(
+                src_ref=mid.at[k],
+                dst_ref=got_z.at[k],
+                send_sem=send_z.at[k],
+                recv_sem=recv_z.at[k],
+                device_id={"seq": lax.rem(s + k, seqs)},
+                device_id_type=MESH,
+            )
+            copy.start()
+            seconds[k] = copy
+        else:
+            out_ref[...] = total
     own.wait()
-    for copy in copies:
+    for copy in smalls:
         copy.wait()
     total = slots[0]
     for index in range(1, count):
         total = total + slots[index]
-    out_ref[...] = total
-
-
-def small_sum(packed):
-    count = lax.axis_size(("seq", "dp"))
-    dp_count = lax.axis_size("dp")
+    small_out[...] = total
+    for k in range(1, seqs):
+        seconds[k].wait_recv()
+        out_ref[...] = out_ref[...] + got_z[k].astype(jnp.float32)
+    for copy in firsts.values():
+        copy.wait_send()
+    for copy in seconds.values():
+        copy.wait_send()
+
+
+def grad_sum(parts, packed):
+    seqs, dps = lax.axis_size("seq"), lax.axis_size("dp")
+    count = seqs * dps
+    block = parts.shape[1:]
+    vmem = pl.BlockSpec(memory_space=pltpu.VMEM)
     return pl.pallas_call(
-        functools.partial(small_sum_kernel, count, dp_count),
-        out_shape=jax.ShapeDtypeStruct(packed.shape, jnp.float32),
-        in_specs=[pl.BlockSpec(memory_space=pltpu.VMEM)],
-        out_specs=pl.BlockSpec(memory_space=pltpu.VMEM),
+        functools.partial(grad_sum_kernel, seqs, dps),
+        out_shape=(
+            jax.ShapeDtypeStruct(block, jnp.float32),
+            jax.ShapeDtypeStruct(packed.shape, jnp.float32),
+        ),
+        in_specs=[vmem, vmem],
+        out_specs=(vmem, vmem),
         scratch_shapes=[
+            pltpu.VMEM((count,) + block, jnp.bfloat16),
+            pltpu.VMEM((seqs,) + block, jnp.bfloat16),
+            pltpu.VMEM((seqs,) + block, jnp.bfloat16),
             pltpu.VMEM((count,) + packed.shape, jnp.float32),
             pltpu.SemaphoreType.DMA,
             pltpu.SemaphoreType.DMA((count,)),
             pltpu.SemaphoreType.DMA((count,)),
+            pltpu.SemaphoreType.DMA((count,)),
+            pltpu.SemaphoreType.DMA((count,)),
+            pltpu.SemaphoreType.DMA((seqs,)),
+            pltpu.SemaphoreType.DMA((seqs,)),
         ],
         compiler_params=pltpu.CompilerParams(
-            collective_id=1, has_side_effects=True, vmem_limit_bytes=16 * 2**20
-        ),
-        cost_estimate=pl.CostEstimate(flops=1000, bytes_accessed=20_000_000, transcendentals=0),
-        name="small_sum",
-    )(packed)
+            collective_id=1, has_side_effects=True, vmem_limit_bytes=32 * 2**20
+        ),
+        cost_estimate=pl.CostEstimate(flops=1000, bytes_accessed=100_000_000, transcendentals=0),
+        name="grad_sum",
+    )(parts, packed)
 
 
 def per_device(
@@ -308,16 +495,27 @@
     hidden_state = inputs.astype(jnp.float32).reshape(rows, width)
     full_first, full_rest = [], []
     for layer in range(layers):
-        first = jnp.concatenate([w_query[layer], w_key[layer], w_value[layer]], 1)
-        rest = jnp.concatenate([w_fc1[layer], w_fc2[layer], w_out[layer]], 1)
-        full_first.append(lax.all_gather(first, group, axis=0, tiled=True))
-        full_rest.append(lax.all_gather(rest, group, axis=0, tiled=True))
+        joined = jnp.concatenate(
+            [
+                w_fc1[layer],
+                w_fc2[layer],
+                w_query[layer],
+                w_key[layer],
+                w_value[layer],
+                w_out[layer],
+            ],
+            1,
+        )
+        if layer == 0:
+            whole = gather_slots(joined, True).reshape(width, joined.shape[1])
+        else:
+            whole = lax.all_gather(joined, group, axis=0, tiled=True)
+        full_first.append(whole[:, 2 * hidden : 2 * hidden + 3 * cols])
+        full_rest.append((whole[:, :hidden], whole[:, hidden : 2 * hidden], whole[:, 2 * hidden + 3 * cols :]))
     saved_all = []
     for layer in range(layers):
         full_qkv = full_first[layer]
-        full_up = full_rest[layer][:, :hidden]
-        full_down = full_rest[layer][:, hidden : 2 * hidden]
-        full_o = full_rest[layer][:, 2 * hidden :]
+        full_up, full_down, full_o = full_rest[layer]
         xhat1, rstd1 = standardize_rows(hidden_state)
         normed1 = (xhat1 * attention_norm_gain[layer] + attention_norm_bias[layer]).astype(
             jnp.bfloat16
@@ -325,8 +523,12 @@
         bias = jnp.concatenate([b_query[layer], jnp.zeros_like(b_query[layer]), b_value[layer]])
         qkv = (matmul(normed1, full_qkv) + bias).astype(jnp.bfloat16)
         queries = qkv[:, :cols].reshape(clips, frames_local, cols)
-        kv_local = qkv[:, cols:].reshape(clips, frames_local, 2 * cols)
-        kv_all = lax.all_gather(kv_local, "seq", axis=1, tiled=True)
+        kv_all = (
+            gather_slots(qkv[:, cols:], False)
+            .reshape(-1, clips, frames_local, 2 * cols)
+            .transpose(1, 0, 2, 3)
+            .reshape(clips, -1, 2 * cols)
+        )
         outcomes = [
             attend_forward(queries[clip], kv_all[clip, :, :cols], kv_all[clip, :, cols:])
             for clip in range(clips)
@@ -348,12 +550,10 @@
         )
     encoded = hidden_state.reshape(clips, frames_local, width)
     state_gradient = cotangent.reshape(rows, width)
-    grads_first, grads_rest, smalls = [None] * layers, [None] * layers, [None] * layers
+    big_grads, smalls = [None] * layers, [None] * layers
     for layer in reversed(range(layers)):
         full_qkv = full_first[layer]
-        full_up = full_rest[layer][:, :hidden]
-        full_down = full_rest[layer][:, hidden : 2 * hidden]
-        full_o = full_rest[layer][:, 2 * hidden :]
+        full_up, full_down, full_o = full_rest[layer]
         (xhat1, rstd1, normed1, queries, kv_all, log_total, attended, xhat2, rstd2, normed2, pre_act, activated) = saved_all[layer]
         grad_mlp = state_gradient.astype(jnp.bfloat16)
         grad_pre = (matmul(grad_mlp, full_down) * gelu_slope(pre_act)).astype(jnp.bfloat16)
@@ -362,15 +562,6 @@
             grad_norm2, xhat2, rstd2, feedforward_norm_gain[layer]
         )
         grad_attn = middle_gradient.astype(jnp.bfloat16)
-        rest_terms = jnp.concatenate(
-            [
-                trans_times(normed2, grad_pre).astype(jnp.bfloat16),
-                trans_times(grad_mlp, activated).astype(jnp.bfloat16),
-                trans_times(grad_attn, attended).astype(jnp.bfloat16),
-            ],
-            1,
-        )
-        grads_rest[layer] = lax.psum_scatter(rest_terms, group, scatter_dimension=0, tiled=True)
         grad_attended = (
             matmul(grad_attn, full_o).astype(jnp.bfloat16).reshape(clips, frames_local, cols)
         )
@@ -385,15 +576,26 @@
             for clip in range(clips)
         ]
         kv_terms = jnp.stack([outcome[1] for outcome in outcomes], 0).astype(jnp.bfloat16)
-        kv_grads = lax.psum_scatter(kv_terms, "seq", scatter_dimension=1, tiled=True)
+        kv_grads = frame_sum(
+            kv_terms.reshape(clips, -1, frames_local, 2 * cols)
+            .transpose(1, 0, 2, 3)
+            .reshape(-1, rows, 2 * cols)
+        )
         grad_query = jnp.concatenate([outcome[0] for outcome in outcomes], 0).astype(jnp.bfloat16)
-        grad_qkv = jnp.concatenate([grad_query, kv_grads.reshape(rows, 2 * cols)], 1)
-        grads_first[layer] = lax.psum_scatter(
-            trans_times(normed1, grad_qkv).astype(jnp.bfloat16),
-            group,
-            scatter_dimension=0,
-            tiled=True,
-        )
+        grad_qkv = jnp.concatenate([grad_query, kv_grads], 1)
+        all_terms = jnp.concatenate(
+            [
+                trans_times(normed2, grad_pre).astype(jnp.bfloat16),
+                trans_times(grad_mlp, activated).astype(jnp.bfloat16),
+                trans_times(normed1, grad_qkv).astype(jnp.bfloat16),
+                trans_times(grad_attn, attended).astype(jnp.bfloat16),
+            ],
+            1,
+        )
+        if layer:
+            big_grads[layer] = lax.psum_scatter(
+                all_terms, group, scatter_dimension=0, tiled=True
+            ).astype(jnp.float32)
         grad_norm1 = tensor_sum(times_trans(grad_qkv, full_qkv))
         state_gradient = middle_gradient + norm_backward_pass(
             grad_norm1, xhat1, rstd1, attention_norm_gain[layer]
@@ -414,7 +616,9 @@
     length = flat.shape[0]
     padded = -(-length // 1024) * 1024
     packed = jnp.pad(flat, (0, padded - length)).reshape(padded // 128, 128)
-    summed = small_sum(packed).reshape(padded)
+    parts = all_terms.reshape(lax.axis_size(group), -1, all_terms.shape[1])
+    big_grads[0], summed = grad_sum(parts, packed)
+    summed = summed.reshape(padded)
     small_stack, offset = [[] for _ in range(9)], 0
     for layer in range(layers):
         for member in range(9):
@@ -422,11 +626,9 @@
             small_stack[member].append(summed[offset : offset + size])
             offset += size
     small_stack = [jnp.stack(members, 0) for members in small_stack]
-    first_out = [grad.astype(jnp.float32) for grad in grads_first]
-    rest_out = [grad.astype(jnp.float32) for grad in grads_rest]
-
-    def pick(parts, start, size):
-        return jnp.stack([part[:, start : start + size] for part in parts], 0)
+
+    def pick(start, size):
+        return jnp.stack([part[:, start : start + size] for part in big_grads], 0)
 
     grad_inputs = state_gradient.reshape(clips, frames_local, width)
     return (
@@ -434,18 +636,18 @@
         grad_inputs,
         small_stack[0],
         small_stack[1],
-        pick(first_out, 0, cols),
+        pick(2 * hidden, cols),
         small_stack[2],
-        pick(first_out, cols, cols),
-        pick(first_out, 2 * cols, cols),
+        pick(2 * hidden + cols, cols),
+        pick(2 * hidden + 2 * cols, cols),
         small_stack[3],
-        pick(rest_out, 2 * hidden, cols),
+        pick(2 * hidden + 3 * cols, cols),
         small_stack[4],
         small_stack[5],
         small_stack[6],
-        pick(rest_out, 0, hidden),
+        pick(0, hidden),
         small_stack[7],
-        pick(rest_out, hidden, hidden),
+        pick(hidden, hidden),
         small_stack[8],
     )
 

time: 594 us -> 503 us (0.85)
  waiting for transfers between devices: 266 us -> 0.04 us
  Pallas kernels: 86.7 us -> 327 us
  blocking collectives: 120 us -> 0 us
  local copies, waits for them, and re-layouts: 28.3 us -> 67.1 us
  matrix products: 39 us -> 49.9 us
    pallas_call x1 -> x6, Pallas kernels: 10.9 us -> 251 us  [the longest x3 133 us: gather_slots(): pl.pallas_call(functools.partial(gather_kernel, seqs, dps, forward), out_...]
    unnamed x10 -> x2, waiting for transfers between devices: 143 us -> 0.03 us
    reduce_scatter x4 -> x1, waiting for transfers between devices: 124 us -> 0.01 us  [per_device(): lax.psum_scatter(all_terms, group, scatter_dimension=0, tiled=True)]
    all_gather x4 -> x0, blocking collectives: 120 us -> none  [the longest x2 74.2 us: per_device(): full_first.append(lax.all_gather(first, group, axis=0, tiled=True))]
    concatenate x0 -> x12, local copies, waits for them, and re-layouts: none -> 25.9 us  [the longest x8 13.1 us: key_side(): jnp.concatenate([grad_key.reshape(frames_all, -1), grad_value.reshape(fra...]
    unnamed x256 -> x191, local copies, waits for them, and re-layouts: 22.3 us -> 11.5 us
  transfers between devices with their start and end apart: 8 -> 2, of which waited for: 6 -> 0; matrix products, arithmetic and copies ran while one was open for 9% -> 13% of each run, Pallas kernels for 7% -> 49%
where the time goes in v2:
time: 503 us; the launch traced here: 494 us
  Pallas kernels  327 us (65%)
  local copies, waits for them, and re-layouts  67.1 us (13%)
  matrix products  49.9 us (10%)
  other arithmetic  34.6 us (7%)
  between operations  15.9 us (3%)
    pallas_call x3, Pallas kernels, gather_slots(): pl.pallas_call(functools.partial(gather_kernel, seqs, dps, forward), out_...  133 us
    pallas_call x8, Pallas kernels, tensor_sum(): pl.pallas_call(tensor_sum_kernel, out_shape=jax.ShapeDtypeStruct((rows, w...  75.6 us
    pallas_call x1, Pallas kernels, grad_sum(): pl.pallas_call(functools.partial(grad_sum_kernel, seqs, dps), out_shape=(...  66.2 us
    pallas_call x2, Pallas kernels, frame_sum(): pl.pallas_call(functools.partial(frame_sum_kernel, seqs), out_shape=jax.S...  51.4 us
    concatenate x8, local copies, waits for them, and re-layouts, key_side(): jnp.concatenate([grad_key.reshape(frames_all, -1), grad_value.reshape(fra...  13.1 us
    dot_general x8, matrix products, matmul(): return jnp.dot(left, right, preferred_element_type=jnp.float32)  12.7 us
    dot_general x8, matrix products, trans_times(): lax.dot_general(left, right, (((0,), (0,)), ((), ())), preferred_element_...  12.2 us
    unnamed x191, local copies, waits for them, and re-layouts  11.5 us
  transfers between devices with their start and end apart: 2, of which 0 were waited for; matrix products, arithmetic and copies ran while one was open for 13% of the time, Pallas kernels for 49%

profile of v2, /device:TPU:0, one launch (start us, length us, event | category | flops | bytes accessed | tf_op | source)
XLA Modules:
  0.0 494.3 jit_solution(14209212146273057727)
XLA Ops:
  13.1 65.2 %gather_weights.1 = bf16[8,96,2304]{2,1,0:T(8,128)(2,1)S(1)} custom-call(bf16[96,2304]{1,0:T(8,128)(2,1)S(1)} %copy-done.4), custom_call_target="tpu_custom_call" | custom-call | flops 1000 | bytes 100000000 | tf_op jit(solution)/shard_map/gather_weights/pallas_call | solution.py:290
  84.7 48.8 %gather_frames.2 = bf16[4,256,384]{2,1,0:T(8,128)(2,1)S(1)} custom-call(bf16[256,384]{1,0:T(8,128)(2,1)S(1)} %slice.343.own_ref), custom_call_target="tpu_custom_call" | custom-call | flops 1000 | bytes 40000000 | tf_op jit(solution)/shard_map/gather_frames/pallas_call | solution.py:290
  144.9 9.6 %tensor_sum.8 = f32[256,768]{1,0:T(8,128)S(1)} custom-call(bf16[256,768]{1,0:T(8,128)(2,1)S(1)} %convolution_convert_fusion.13.part_ref), custom_call_target="tpu_custom_call" | custom-call | flops 786432 | bytes 20000000 | tf_op jit(solution)/shard_map/tensor_sum/pallas_call | solution.py:204
  156.8 2.9 fusion.71
  161.0 9.6 %tensor_sum.9 = f32[256,768]{1,0:T(8,128)S(1)} custom-call(bf16[256,768]{1,0:T(8,128)(2,1)S(1)} %convolution_convert_fusion.12.part_ref), custom_call_target="tpu_custom_call" | custom-call | flops 786432 | bytes 20000000 | tf_op jit(solution)/shard_map/tensor_sum/pallas_call | solution.py:204
  175.3 19.4 %gather_frames.3 = bf16[4,256,384]{2,1,0:T(8,128)(2,1)S(1)} custom-call(bf16[256,384]{1,0:T(8,128)(2,1)S(1)} %slice.351.own_ref), custom_call_target="tpu_custom_call" | custom-call | flops 1000 | bytes 40000000 | tf_op jit(solution)/shard_map/gather_frames/pallas_call | solution.py:290
  206.4 2.9 fusion.38
  209.9 8.7 %tensor_sum.10 = f32[256,768]{1,0:T(8,128)S(1)} custom-call(bf16[256,768]{1,0:T(8,128)(2,1)S(1)} %convolution_convert_fusion.11.part_ref), custom_call_target="tpu_custom_call" | custom-call | flops 786432 | bytes 20000000 | tf_op jit(solution)/shard_map/tensor_sum/pallas_call | solution.py:204
  219.1 2.1 fusion.74
  221.7 9.6 %tensor_sum.11 = f32[256,768]{1,0:T(8,128)S(1)} custom-call(bf16[256,768]{1,0:T(8,128)(2,1)S(1)} %convolution_convert_fusion.10.part_ref), custom_call_target="tpu_custom_call" | custom-call | flops 786432 | bytes 20000000 | tf_op jit(solution)/shard_map/tensor_sum/pallas_call | solution.py:204
  233.0 9.6 %tensor_sum.12 = f32[256,768]{1,0:T(8,128)S(1)} custom-call(bf16[256,768]{1,0:T(8,128)(2,1)S(1)} %convolution_convert_fusion.9.part_ref), custom_call_target="tpu_custom_call" | custom-call | flops 786432 | bytes 20000000 | tf_op jit(solution)/shard_map/tensor_sum/pallas_call | solution.py:204
  256.2 2.1 concatenate.51
  260.3 2.1 concatenate.52
  264.4 2.4 pad_maximum_fusion.1.part_ref
  269.6 20.4 %frame_sum.2 = bf16[256,384]{1,0:T(8,128)(2,1)S(1)} custom-call(bf16[4,256,384]{2,1,0:T(8,128)(2,1)S(1)} %copy-done.3), custom_call_target="tpu_custom_call" | custom-call | flops 1000 | bytes 40000000 | tf_op jit(solution)/shard_map/frame_sum/pallas_call | solution.py:339
  290.1 2.9 convolution_convert_fusion.4
  294.8 9.6 %tensor_sum.13 = f32[256,768]{1,0:T(8,128)S(1)} custom-call(bf16[256,768]{1,0:T(8,128)(2,1)S(1)} %convolution_convert_fusion.8.part_ref), custom_call_target="tpu_custom_call" | custom-call | flops 786432 | bytes 20000000 | tf_op jit(solution)/shard_map/tensor_sum/pallas_call | solution.py:204
  308.7 9.6 %tensor_sum.14 = f32[256,768]{1,0:T(8,128)S(1)} custom-call(bf16[256,768]{1,0:T(8,128)(2,1)S(1)} %convolution_convert_fusion.7.part_ref), custom_call_target="tpu_custom_call" | custom-call | flops 786432 | bytes 20000000 | tf_op jit(solution)/shard_map/tensor_sum/pallas_call | solution.py:204
  325.0 6.7 %concatenate.61 = bf16[768,2304]{1,0:T(8,128)(2,1)} concatenate(bf16[768,768]{1,0:T(8,128)(2,1)} %convolution_convert_fusion.1, bf16[768,768]{1,0:T(8,128)(2,1)} %fusion.14, bf16[768,576]{1,0:T(8,128)(2,1)S(1)} %copy.91, bf16[768,192]{1,0:T(8,128)(2,1)S(1)} %copy.92), dimensions={1} | concatenate | bytes 7077888 | tf_op jit(solution)/shard_map/concatenate | solution.py:586
  341.0 2.4 fusion.28
  347.5 30.9 %frame_sum.3 = bf16[256,384]{1,0:T(8,128)(2,1)S(1)} custom-call(bf16[4,256,384]{2,1,0:T(8,128)(2,1)S(1)} %pad_maximum_fusion.2.part_ref), custom_call_target="tpu_custom_call" | custom-call | flops 1000 | bytes 40000000 | tf_op jit(solution)/shard_map/frame_sum/pallas_call | solution.py:339
  386.3 4.4 copy.88
  392.9 9.5 %tensor_sum.15 = f32[256,768]{1,0:T(8,128)S(1)} custom-call(bf16[256,768]{1,0:T(8,128)(2,1)S(1)} %convolution_convert_fusion.6.part_ref), custom_call_target="tpu_custom_call" | custom-call | flops 786432 | bytes 20000000 | tf_op jit(solution)/shard_map/tensor_sum/pallas_call | solution.py:204
  408.0 66.2 %grad_sum.1 = (f32[96,2304]{1,0:T(8,128)S(1)}, f32[96,128]{1,0:T(8,128)S(1)}) custom-call(bf16[8,96,2304]{2,1,0:T(8,128)(2,1)S(1)} %bitcast.292, f32[96,128]{1,0:T(8,128)S(1)} %pad_bitcast_fusion.small_ref), custom_call_target="tpu_custom_call" | custom-call | flops 1000 | bytes 100000000 | tf_op jit(solution)/shard_map/grad_sum/pallas_call | solution.py:441
  (330 shorter events, 120.9 us)
Async XLA Ops:
  7.2 165.3 %all-gather.2.cloned.1.call-start = ((), (), s32[]{:S(2)}) async-start(), calls=%async_computation.1 | async-start | bytes 3981312 | tf_op jit(solution)/shard_map/all_gather | solution.py:512
  10.2 68.9 %copy-start.75 = (f32[2,768]{1,0:T(2,128)S(1)}, f32[2,768]{1,0:T(2,128)}, u32[]{:S(2)}) copy-start(f32[2,768]{1,0:T(2,128)} %param.20) | copy-start | bytes 18436
  11.1 470.2 %reduce-scatter.2.cloned.1.call-start = ((), (), s32[]{:S(2)}) async-start(), calls=%async_computation.2 | async-start | bytes 3981312 | tf_op jit(solution)/shard_map/reduce_scatter | solution.py:596
  78.3 241.9 %copy-start.2 = (bf16[8,96,2304]{2,1,0:T(8,128)(2,1)}, bf16[8,96,2304]{2,1,0:T(8,128)(2,1)S(1)}, u32[]{:S(2)}) copy-start(bf16[8,96,2304]{2,1,0:T(8,128)(2,1)S(1)} %gather_weights.1) | copy-start | bytes 10616836
  80.5 54.8 %copy-start.48 = (f32[768]{0:T(1024)}, f32[768]{0:T(1024)S(1)}, u32[]{:S(2)}) copy-start(f32[768]{0:T(1024)S(1)} %get-tuple-element.143) | copy-start | bytes 9220
  144.4 15.3 %copy-start.43 = (bf16[3,64,256]{2,1,0:T(8,128)(2,1)}, bf16[3,64,256]{2,1,0:T(8,128)(2,1)S(1)}, u32[]{:S(2)}) copy-start(bf16[3,64,256]{2,1,0:T(8,128)(2,1)S(1)} %fusion.39) | copy-start | bytes 294916
  256.2 33.9 %copy-start.54 = (f32[256]{0:T(256)S(1)}, f32[256]{0:T(256)}, u32[]{:S(2)}) copy-start(f32[256]{0:T(256)} %copy-done.53) | copy-start | bytes 3076
  269.6 34.8 %copy-start.18 = (f32[256,768]{1,0:T(8,128)S(1)}, f32[256,768]{1,0:T(8,128)}, u32[]{:S(2)}) copy-start(f32[256,768]{1,0:T(8,128)} %copy-done.16) | copy-start | bytes 2359300
  269.6 34.8 %copy-start.65 = (f32[256]{0:T(256)S(1)}, f32[256]{0:T(256)}, u32[]{:S(2)}) copy-start(f32[256]{0:T(256)} %add_rsqrt_fusion.1) | copy-start | bytes 3076
  290.1 15.2 %copy-start.25 = (f32[256,768]{1,0:T(8,128)S(1)}, f32[256,768]{1,0:T(8,128)}, u32[]{:S(2)}) copy-start(f32[256,768]{1,0:T(8,128)} %copy-done.24) | copy-start | bytes 2359300
  343.4 35.0 %copy-start.20 = (bf16[3,256,1024]{2,1,0:T(8,128)(2,1)S(1)}, bf16[3,256,1024]{2,1,0:T(8,128)(2,1)}, u32[]{:S(2)}) copy-start(bf16[3,256,1024]{2,1,0:T(8,128)(2,1)} %copy-done.19) | copy-start | bytes 4718596
  343.4 35.0 %copy-start.31 = (bf16[1,1024,192]{1,2,0:T(8,128)(2,1)S(1)}, bf16[1,1024,192]{1,2,0:T(8,128)(2,1)}, u32[]{:S(2)}) copy-start(bf16[1,1024,192]{1,2,0:T(8,128)(2,1)} %copy.77) | copy-start | bytes 1179652
  344.8 34.4 %copy-start.22 = (f32[256,768]{1,0:T(8,128)S(1)}, f32[256,768]{1,0:T(8,128)}, u32[]{:S(2)}) copy-start(f32[256,768]{1,0:T(8,128)} %copy-done.21) | copy-start | bytes 2359300
  344.8 34.4 %copy-start.44 = (bf16[3,64,256]{2,1,0:T(8,128)(2,1)S(1)}, bf16[3,64,256]{2,1,0:T(8,128)(2,1)}, u32[]{:S(2)}) copy-start(bf16[3,64,256]{2,1,0:T(8,128)(2,1)} %copy-done.43) | copy-start | bytes 294916
  345.9 33.6 %copy-start.27 = (bf16[1,256,768]{2,1,0:T(8,128)(2,1)S(1)}, bf16[1,256,768]{2,1,0:T(8,128)(2,1)}, u32[]{:S(2)}) copy-start(bf16[1,256,768]{2,1,0:T(8,128)(2,1)} %param.17) | copy-start | bytes 1179652
  345.9 33.6 %copy-start.49 = (f32[768]{0:T(1024)S(1)}, f32[768]{0:T(1024)}, u32[]{:S(2)}) copy-start(f32[768]{0:T(1024)} %copy-done.48) | copy-start | bytes 9220
  345.9 33.6 %copy-start.59 = (f32[256]{0:T(256)S(1)}, f32[256]{0:T(256)}, u32[]{:S(2)}) copy-start(f32[256]{0:T(256)} %copy-done.58) | copy-start | bytes 3076
  407.0 72.9 %copy-start.82 = (f32[256]{0:T(256)S(1)}, f32[256]{0:T(256)}, u32[]{:S(2)}) copy-start(f32[256]{0:T(256)} %get-tuple-element.28) | copy-start | bytes 3076
  407.0 72.9 %copy-start.81 = (f32[256]{0:T(256)S(1)}, f32[256]{0:T(256)}, u32[]{:S(2)}) copy-start(f32[256]{0:T(256)} %get-tuple-element.29) | copy-start | bytes 3076
  407.0 73.1 %copy-start.1 = (f32[256,768]{1,0:T(8,128)S(1)}, f32[256,768]{1,0:T(8,128)}, u32[]{:S(2)}) copy-start(f32[256,768]{1,0:T(8,128)} %copy-done) | copy-start | bytes 2359300
  407.0 73.1 %copy-start.23 = (f32[256,768]{1,0:T(8,128)S(1)}, f32[256,768]{1,0:T(8,128)}, u32[]{:S(2)}) copy-start(f32[256,768]{1,0:T(8,128)} %copy-done.21) | copy-start | bytes 2359300
  407.0 73.1 %copy-start.29 = (bf16[1,256,768]{2,1,0:T(8,128)(2,1)S(1)}, bf16[1,256,768]{2,1,0:T(8,128)(2,1)}, u32[]{:S(2)}) copy-start(bf16[1,256,768]{2,1,0:T(8,128)(2,1)} %param.17) | copy-start | bytes 1179652
  407.0 73.1 %copy-start.61 = (f32[256]{0:T(256)S(1)}, f32[256]{0:T(256)}, u32[]{:S(2)}) copy-start(f32[256]{0:T(256)} %copy-done.58) | copy-start | bytes 3076
  407.0 73.1 %copy-start.74 = (f32[256]{0:T(256)S(1)}, f32[256]{0:T(256)}, u32[]{:S(2)}) copy-start(f32[256]{0:T(256)} %copy-done.72) | copy-start | bytes 3076
  (66 other events, 435.6 us)
Sparse Core Ops, SparseCore 0:
  11.2 107.4 all-gather.1
  331.8 115.7 reduce-scatter.1

commit v3 on v2

--- a/solution.py
+++ b/solution.py
@@ -54,73 +54,84 @@
     )
 
 
-def split_heads(block):
-    return block.reshape(block.shape[0], block.shape[1] // HEAD_DIM, HEAD_DIM)
-
-
-def attend_forward(query_blk, key_blk, value_blk):
+def attend_forward_kernel(query_ref, pair_ref, out_ref, log_ref):
+    cols = query_ref.shape[1]
     scale = HEAD_DIM ** (-0.5)
-    scores = (
-        jnp.einsum(
-            "qhd,khd->hqk",
-            split_heads(query_blk),
-            split_heads(key_blk),
-            preferred_element_type=jnp.float32,
-        )
-        * scale
-    )
-    top = jnp.max(scores, -1, keepdims=True)
-    expo = jnp.exp(scores - top)
-    total = jnp.sum(expo, -1, keepdims=True)
-    prob = (expo / total).astype(jnp.bfloat16)
-    attended = jnp.einsum(
-        "hqk,khd->qhd", prob, split_heads(value_blk), preferred_element_type=jnp.float32
-    )
-    attended = attended.reshape(query_blk.shape[0], -1).astype(jnp.bfloat16)
-    return (attended, (top + jnp.log(total))[..., 0])
-
-
-def score_grads(query_heads, key_heads, value_heads, log_total, grad_heads, inner):
+    query_blk, pair_blk = query_ref[...], pair_ref[...]
+    outcomes = []
+    for head in range(cols // HEAD_DIM):
+        low, high = head * HEAD_DIM, (head + 1) * HEAD_DIM
+        scores = times_trans(query_blk[:, low:high], pair_blk[:, low:high]) * scale
+        top = jnp.max(scores, -1, keepdims=True)
+        expo = jnp.exp(scores - top)
+        total = jnp.sum(expo, -1, keepdims=True)
+        prob = (expo / total).astype(jnp.bfloat16)
+        outcomes.append(matmul(prob, pair_blk[:, cols + low : cols + high]))
+        log_ref[head] = top + jnp.log(total)
+    out_ref[...] = jnp.concatenate(outcomes, 1).astype(jnp.bfloat16)
+
+
+def attend_backward_kernel(query_ref, pair_ref, log_ref, grad_ref, grad_query_ref, grad_pair_ref):
+    cols = query_ref.shape[1]
     scale = HEAD_DIM ** (-0.5)
-    scores = (
-        jnp.einsum("qhd,khd->hqk", query_heads, key_heads, preferred_element_type=jnp.float32)
-        * scale
-    )
-    prob = jnp.exp(scores - log_total[..., None])
-    grad_prob = jnp.einsum(
-        "qhd,khd->hqk", grad_heads, value_heads, preferred_element_type=jnp.float32
-    )
-    inner = jnp.sum(prob * grad_prob, -1)
-    grad_scores = (prob * (grad_prob - inner[..., None])).astype(jnp.bfloat16)
-    return (prob, grad_scores, inner)
-
-
-def key_side(grad_scores, prob, query_heads, grad_heads, frames_all):
-    scale = HEAD_DIM ** (-0.5)
-    grad_key = (
-        jnp.einsum("hqk,qhd->khd", grad_scores, query_heads, preferred_element_type=jnp.float32)
-        * scale
-    )
-    grad_value = jnp.einsum(
-        "hqk,qhd->khd", prob.astype(jnp.bfloat16), grad_heads, preferred_element_type=jnp.float32
-    )
-    return jnp.concatenate(
-        [grad_key.reshape(frames_all, -1), grad_value.reshape(frames_all, -1)], 1
-    )
-
-
-def attend_backward(query_blk, key_blk, value_blk, log_total, grad_blk):
-    query_heads = split_heads(query_blk)
-    key_heads = split_heads(key_blk)
-    grad_heads = split_heads(grad_blk)
-    prob, grad_scores, inner = score_grads(
-        query_heads, key_heads, split_heads(value_blk), log_total, grad_heads, None
-    )
-    grad_query = jnp.einsum(
-        "hqk,khd->qhd", grad_scores, key_heads, preferred_element_type=jnp.float32
-    ) * HEAD_DIM ** (-0.5)
-    joined = key_side(grad_scores, prob, query_heads, grad_heads, key_blk.shape[0])
-    return (grad_query.reshape(query_blk.shape[0], -1), joined)
+    query_blk, pair_blk, grad_blk = query_ref[...], pair_ref[...], grad_ref[...]
+    grad_queries, grad_keys, grad_values = [], [], []
+    for head in range(cols // HEAD_DIM):
+        low, high = head * HEAD_DIM, (head + 1) * HEAD_DIM
+        query_head, key_head = query_blk[:, low:high], pair_blk[:, low:high]
+        grad_head, value_head = grad_blk[:, low:high], pair_blk[:, cols + low : cols + high]
+        scores = times_trans(query_head, key_head) * scale
+        prob = jnp.exp(scores - log_ref[head])
+        grad_prob = times_trans(grad_head, value_head)
+        inner = jnp.sum(prob * grad_prob, -1, keepdims=True)
+        grad_scores = (prob * (grad_prob - inner)).astype(jnp.bfloat16)
+        grad_queries.append(matmul(grad_scores, key_head) * scale)
+        grad_keys.append(trans_times(grad_scores, query_head) * scale)
+        grad_values.append(trans_times(prob.astype(jnp.bfloat16), grad_head))
+    grad_query_ref[...] = jnp.concatenate(grad_queries, 1).astype(jnp.bfloat16)
+    grad_pair_ref[...] = jnp.concatenate(grad_keys + grad_values, 1).astype(jnp.bfloat16)
+
+
+def attend_forward(query_blk, pair_blk):
+    frames, cols = query_blk.shape
+    vmem = pl.BlockSpec(memory_space=pltpu.VMEM)
+    return pl.pallas_call(
+        attend_forward_kernel,
+        out_shape=(
+            jax.ShapeDtypeStruct((frames, cols), jnp.bfloat16),
+            jax.ShapeDtypeStruct((cols // HEAD_DIM, frames, 1), jnp.float32),
+        ),
+        in_specs=[vmem, vmem],
+        out_specs=(vmem, vmem),
+        compiler_params=pltpu.CompilerParams(vmem_limit_bytes=32 * 2**20),
+        cost_estimate=pl.CostEstimate(
+            flops=4 * frames * pair_blk.shape[0] * cols,
+            bytes_accessed=15_000_000,
+            transcendentals=0,
+        ),
+        name="attend_forward",
+    )(query_blk, pair_blk)
+
+
+def attend_backward(query_blk, pair_blk, log_total, grad_blk):
+    frames, cols = query_blk.shape
+    vmem = pl.BlockSpec(memory_space=pltpu.VMEM)
+    return pl.pallas_call(
+        attend_backward_kernel,
+        out_shape=(
+            jax.ShapeDtypeStruct((frames, cols), jnp.bfloat16),
+            jax.ShapeDtypeStruct(pair_blk.shape, jnp.bfloat16),
+        ),
+        in_specs=[vmem] * 4,
+        out_specs=(vmem, vmem),
+        compiler_params=pltpu.CompilerParams(vmem_limit_bytes=32 * 2**20),
+        cost_estimate=pl.CostEstimate(
+            flops=10 * frames * pair_blk.shape[0] * cols,
+            bytes_accessed=20_000_000,
+            transcendentals=0,
+        ),
+        name="attend_backward",
+    )(query_blk, pair_blk, log_total, grad_blk)
 
 
 MESH = pl.DeviceIdType.MESH
@@ -507,8 +518,11 @@
             1,
         )
         if layer == 0:
-            whole = gather_slots(joined, True).reshape(width, joined.shape[1])
+            whole = gather_slots(joined, True)
+            last = whole
+            whole = whole.reshape(width, joined.shape[1])
         else:
+            joined = joined + last[0, :1, :1] * 0
             whole = lax.all_gather(joined, group, axis=0, tiled=True)
         full_first.append(whole[:, 2 * hidden : 2 * hidden + 3 * cols])
         full_rest.append((whole[:, :hidden], whole[:, hidden : 2 * hidden], whole[:, 2 * hidden + 3 * cols :]))
@@ -530,7 +544,7 @@
             .reshape(clips, -1, 2 * cols)
         )
         outcomes = [
-            attend_forward(queries[clip], kv_all[clip, :, :cols], kv_all[clip, :, cols:])
+            attend_forward(queries[clip], kv_all[clip])
             for clip in range(clips)
         ]
         log_total = [outcome[1] for outcome in outcomes]
@@ -568,8 +582,7 @@
         outcomes = [
             attend_backward(
                 queries[clip],
-                kv_all[clip, :, :cols],
-                kv_all[clip, :, cols:],
+                kv_all[clip],
                 log_total[clip],
                 grad_attended[clip],
             )
@@ -592,11 +605,13 @@
             ],
             1,
         )
+        back_terms = times_trans(grad_qkv, full_qkv).astype(jnp.bfloat16)
         if layer:
+            back_terms = back_terms + all_terms[:1, :1] * 0
             big_grads[layer] = lax.psum_scatter(
                 all_terms, group, scatter_dimension=0, tiled=True
             ).astype(jnp.float32)
-        grad_norm1 = tensor_sum(times_trans(grad_qkv, full_qkv))
+        grad_norm1 = tensor_sum(back_terms)
         state_gradient = middle_gradient + norm_backward_pass(
             grad_norm1, xhat1, rstd1, attention_norm_gain[layer]
         )

time: 503 us -> 439 us (0.87)
  local copies, waits for them, and re-layouts: 67.1 us -> 34.9 us
  Pallas kernels: 327 us -> 303 us
  matrix products: 49.9 us -> 31.4 us
  waiting for transfers between devices: 0.04 us -> 16.3 us
  other arithmetic: 34.6 us -> 29.1 us
    pallas_call x3, Pallas kernels: 133 us -> 107 us  [gather_slots(): pl.pallas_call(functools.partial(gather_kernel, seqs, dps, forward), out_...]
    dot_general x12 -> x0, matrix products: 18.2 us -> none  [the longest x2 3.85 us: key_side(): jnp.einsum('hqk,qhd->khd', prob.astype(jnp.bfloat16), grad_heads, preferr...]
    all_gather x1, waiting for transfers between devices: 0.01 us -> 16.3 us  [per_device(): whole = lax.all_gather(joined, group, axis=0, tiled=True)]
    concatenate x8 -> x0, local copies, waits for them, and re-layouts: 13.1 us -> none  [key_side(): jnp.concatenate([grad_key.reshape(frames_all, -1), grad_value.reshape(fra...]
    pallas_call x0 -> x4, Pallas kernels: none -> 10.6 us  [the longest x2 6.28 us: attend_backward(): pl.pallas_call(attend_backward_kernel, out_shape=(jax.ShapeDtypeStruct((f...]
    slice x6 -> x2, local copies, waits for them, and re-layouts: 10.3 us -> 1.75 us  [the longest x1 1.2 us: per_device(): back_terms = back_terms + all_terms[:1, :1] * 0]
    unnamed x191 -> x147, local copies, waits for them, and re-layouts: 11.5 us -> 3.28 us
    pallas_call x1, Pallas kernels: 66.2 us -> 59 us  [grad_sum(): pl.pallas_call(functools.partial(grad_sum_kernel, seqs, dps), out_shape=(...]
  transfers between devices with their start and end apart: 2 -> 2, of which waited for: 0 -> 1; matrix products, arithmetic and copies ran while one was open for 13% -> 11% of each run, Pallas kernels for 49% -> 41%
where the time goes in v3:
time: 439 us; the launch traced here: 432 us
  Pallas kernels  303 us (69%)
  local copies, waits for them, and re-layouts  34.9 us (8%)
  matrix products  31.4 us (7%)
  other arithmetic  29.1 us (7%)
  between operations  17.1 us (4%)
  waiting for transfers between devices  16.3 us (4%)
    pallas_call x3, Pallas kernels, gather_slots(): pl.pallas_call(functools.partial(gather_kernel, seqs, dps, forward), out_...  107 us
    pallas_call x8, Pallas kernels, tensor_sum(): pl.pallas_call(tensor_sum_kernel, out_shape=jax.ShapeDtypeStruct((rows, w...  75.9 us
    pallas_call x1, Pallas kernels, grad_sum(): pl.pallas_call(functools.partial(grad_sum_kernel, seqs, dps), out_shape=(...  59 us
    pallas_call x2, Pallas kernels, frame_sum(): pl.pallas_call(functools.partial(frame_sum_kernel, seqs), out_shape=jax.S...  50.5 us
    all_gather x1, waiting for transfers between devices, per_device(): whole = lax.all_gather(joined, group, axis=0, tiled=True)  16.3 us
    dot_general x8, matrix products, matmul(): return jnp.dot(left, right, preferred_element_type=jnp.float32)  15.7 us
    concatenate x2, local copies, waits for them, and re-layouts, per_device(): jnp.concatenate([trans_times(normed2, grad_pre).astype(jnp.bfloat16), tra...  11.2 us
  transfers between devices with their start and end apart: 2, of which 1 were waited for; matrix products, arithmetic and copies ran while one was open for 11% of the time, Pallas kernels for 41%

profile of v3, /device:TPU:0, one launch (start us, length us, event | category | flops | bytes accessed | tf_op | source)
XLA Modules:
  0.0 432.0 jit_solution(8203591023741279159)
XLA Ops:
  14.0 47.5 %gather_weights.1 = bf16[8,96,2304]{2,1,0:T(8,128)(2,1)S(1)} custom-call(bf16[96,2304]{1,0:T(8,128)(2,1)S(1)} %copy-done.5), custom_call_target="tpu_custom_call" | custom-call | flops 1000 | bytes 100000000 | tf_op jit(solution)/shard_map/gather_weights/pallas_call | solution.py:301
  73.0 43.3 %gather_frames.2 = bf16[4,256,384]{2,1,0:T(8,128)(2,1)S(1)} custom-call(bf16[256,384]{1,0:T(8,128)(2,1)S(1)} %slice.332.own_ref), custom_call_target="tpu_custom_call" | custom-call | flops 1000 | bytes 40000000 | tf_op jit(solution)/shard_map/gather_frames/pallas_call | solution.py:301
  116.3 2.2 attend_forward.2
  118.9 9.6 %tensor_sum.8 = f32[256,768]{1,0:T(8,128)S(1)} custom-call(bf16[256,768]{1,0:T(8,128)(2,1)S(1)} %convolution_convert_fusion.13.part_ref), custom_call_target="tpu_custom_call" | custom-call | flops 786432 | bytes 20000000 | tf_op jit(solution)/shard_map/tensor_sum/pallas_call | solution.py:215
  130.8 2.9 fusion.38
  135.1 9.6 %tensor_sum.9 = f32[256,768]{1,0:T(8,128)S(1)} custom-call(bf16[256,768]{1,0:T(8,128)(2,1)S(1)} %convolution_convert_fusion.12.part_ref), custom_call_target="tpu_custom_call" | custom-call | flops 786432 | bytes 20000000 | tf_op jit(solution)/shard_map/tensor_sum/pallas_call | solution.py:215
  145.1 16.3 %all-gather.2.cloned.1.call-done = bf16[768,2304]{1,0:T(8,128)(2,1)} async-done(((bf16[96,2304]{1,0:T(8,128)(2,1)}), bf16[768,2304]{1,0:T(8,128)(2,1)}) %all-gather.2.cloned.1.call-update) | async-done | bytes 3538960 | tf_op jit(solution)/shard_map/all_gather | solution.py:526
  163.4 16.3 %gather_frames.3 = bf16[4,256,384]{2,1,0:T(8,128)(2,1)S(1)} custom-call(bf16[256,384]{1,0:T(8,128)(2,1)S(1)} %slice.338.own_ref), custom_call_target="tpu_custom_call" | custom-call | flops 1000 | bytes 40000000 | tf_op jit(solution)/shard_map/gather_frames/pallas_call | solution.py:301
  182.3 9.6 %tensor_sum.10 = f32[256,768]{1,0:T(8,128)S(1)} custom-call(bf16[256,768]{1,0:T(8,128)(2,1)S(1)} %convolution_convert_fusion.11.part_ref), custom_call_target="tpu_custom_call" | custom-call | flops 786432 | bytes 20000000 | tf_op jit(solution)/shard_map/tensor_sum/pallas_call | solution.py:215
  194.9 9.6 %tensor_sum.11 = f32[256,768]{1,0:T(8,128)S(1)} custom-call(bf16[256,768]{1,0:T(8,128)(2,1)S(1)} %convolution_convert_fusion.10.part_ref), custom_call_target="tpu_custom_call" | custom-call | flops 786432 | bytes 20000000 | tf_op jit(solution)/shard_map/tensor_sum/pallas_call | solution.py:215
  209.5 9.6 %tensor_sum.12 = f32[256,768]{1,0:T(8,128)S(1)} custom-call(bf16[256,768]{1,0:T(8,128)(2,1)S(1)} %convolution_convert_fusion.9.part_ref), custom_call_target="tpu_custom_call" | custom-call | flops 786432 | bytes 20000000 | tf_op jit(solution)/shard_map/tensor_sum/pallas_call | solution.py:215
  222.8 3.2 attend_backward.2
  226.0 20.6 %frame_sum.2 = bf16[256,384]{1,0:T(8,128)(2,1)S(1)} custom-call(bf16[4,256,384]{2,1,0:T(8,128)(2,1)S(1)} %bitcast.253), custom_call_target="tpu_custom_call" | custom-call | flops 1000 | bytes 40000000 | tf_op jit(solution)/shard_map/frame_sum/pallas_call | solution.py:350
  251.8 9.0 %tensor_sum.13 = f32[256,768]{1,0:T(8,128)S(1)} custom-call(bf16[256,768]{1,0:T(8,128)(2,1)S(1)} %fusion.6.part_ref), custom_call_target="tpu_custom_call" | custom-call | flops 786432 | bytes 20000000 | tf_op jit(solution)/shard_map/tensor_sum/pallas_call | solution.py:215
  261.8 2.2 copy.50
  264.2 6.7 %concatenate.35 = bf16[768,2304]{1,0:T(8,128)(2,1)} concatenate(bf16[768,768]{1,0:T(8,128)(2,1)} %convolution_convert_fusion.3, bf16[768,768]{1,0:T(8,128)(2,1)} %fusion, bf16[768,576]{1,0:T(8,128)(2,1)} %copy.50, bf16[768,192]{1,0:T(8,128)(2,1)S(1)} %copy.51), dimensions={1} | concatenate | bytes 7077888 | tf_op jit(solution)/shard_map/concatenate | solution.py:599
  271.8 3.0 convert_reduce_fusion.5
  277.3 9.6 %tensor_sum.14 = f32[256,768]{1,0:T(8,128)S(1)} custom-call(bf16[256,768]{1,0:T(8,128)(2,1)S(1)} %convolution_convert_fusion.7.part_ref), custom_call_target="tpu_custom_call" | custom-call | flops 786432 | bytes 20000000 | tf_op jit(solution)/shard_map/tensor_sum/pallas_call | solution.py:215
  288.8 2.5 convolution_convert_fusion.16
  292.3 3.0 attend_backward.3
  295.4 29.9 %frame_sum.3 = bf16[256,384]{1,0:T(8,128)(2,1)S(1)} custom-call(bf16[4,256,384]{2,1,0:T(8,128)(2,1)S(1)} %bitcast.254), custom_call_target="tpu_custom_call" | custom-call | flops 1000 | bytes 40000000 | tf_op jit(solution)/shard_map/frame_sum/pallas_call | solution.py:350
  330.6 4.6 %copy.48 = bf16[768,2304]{1,0:T(8,128)(2,1)S(1)} copy(bf16[768,2304]{0,1:T(8,128)(2,1)} %pad_maximum_fusion) | data formatting | bytes 7077888 | tf_op jit(solution)/shard_map/concatenate | solution.py:599
  337.3 9.6 %tensor_sum.15 = f32[256,768]{1,0:T(8,128)S(1)} custom-call(bf16[256,768]{1,0:T(8,128)(2,1)S(1)} %convolution_convert_fusion.6.part_ref), custom_call_target="tpu_custom_call" | custom-call | flops 786432 | bytes 20000000 | tf_op jit(solution)/shard_map/tensor_sum/pallas_call | solution.py:215
  353.0 59.0 %grad_sum.1 = (f32[96,2304]{1,0:T(8,128)S(1)}, f32[96,128]{1,0:T(8,128)S(1)}) custom-call(bf16[8,96,2304]{2,1,0:T(8,128)(2,1)S(1)} %bitcast.240, f32[96,128]{1,0:T(8,128)S(1)} %pad_bitcast_fusion.small_ref), custom_call_target="tpu_custom_call" | custom-call | flops 1000 | bytes 100000000 | tf_op jit(solution)/shard_map/grad_sum/pallas_call | solution.py:452
  (257 shorter events, 75.9 us)
Async XLA Ops:
  7.2 154.2 %all-gather.2.cloned.1.call-start = ((), (), s32[]{:S(2)}) async-start(), calls=%async_computation.1 | async-start | bytes 3981312 | tf_op jit(solution)/shard_map/all_gather | solution.py:526
  12.1 54.5 %copy-start.64 = (f32[2,192]{1,0:T(2,128)S(1)}, f32[2,192]{1,0:T(2,128)}, u32[]{:S(2)}) copy-start(f32[2,192]{1,0:T(2,128)} %param.22) | copy-start | bytes 4612
  12.1 54.5 %copy-start.65 = (f32[2,192]{1,0:T(2,128)S(1)}, f32[2,192]{1,0:T(2,128)}, u32[]{:S(2)}) copy-start(f32[2,192]{1,0:T(2,128)} %param.25) | copy-start | bytes 4612
  61.6 72.2 %copy-start.2 = (bf16[8,96,2304]{2,1,0:T(8,128)(2,1)}, bf16[8,96,2304]{2,1,0:T(8,128)(2,1)S(1)}, u32[]{:S(2)}) copy-start(bf16[8,96,2304]{2,1,0:T(8,128)(2,1)S(1)} %gather_weights.1) | copy-start | bytes 10616836
  66.6 352.5 %reduce-scatter.2.cloned.1.call-start = ((), (), s32[]{:S(2)}) async-start(), calls=%async_computation.2 | async-start | bytes 3981312 | tf_op jit(solution)/shard_map/reduce_scatter | solution.py:611
  68.8 47.6 %copy-start.61 = (f32[768]{0:T(1024)}, f32[768]{0:T(1024)S(1)}, u32[]{:S(2)}) copy-start(f32[768]{0:T(1024)S(1)} %get-tuple-element.66) | copy-start | bytes 9220
  69.9 58.6 %copy-start.39 = (f32[256]{0:T(256)}, f32[256]{0:T(256)S(1)}, u32[]{:S(2)}) copy-start(f32[256]{0:T(256)S(1)} %broadcast_multiply_fusion.11) | copy-start | bytes 3076
  71.2 57.3 %copy-start.51 = (f32[256]{0:T(256)}, f32[256]{0:T(256)S(1)}, u32[]{:S(2)}) copy-start(f32[256]{0:T(256)S(1)} %add_rsqrt_fusion.3) | copy-start | bytes 3076
  71.2 57.3 %copy-start.54 = (f32[2,768]{1,0:T(2,128)S(1)}, f32[2,768]{1,0:T(2,128)}, u32[]{:S(2)}) copy-start(f32[2,768]{1,0:T(2,128)} %param.27) | copy-start | bytes 18436
  71.2 57.9 %copy-start.55 = (f32[2,768]{1,0:T(2,128)S(1)}, f32[2,768]{1,0:T(2,128)}, u32[]{:S(2)}) copy-start(f32[2,768]{1,0:T(2,128)} %param.33) | copy-start | bytes 18436
  71.2 57.9 %copy-start.56 = (f32[2,768]{1,0:T(2,128)S(1)}, f32[2,768]{1,0:T(2,128)}, u32[]{:S(2)}) copy-start(f32[2,768]{1,0:T(2,128)} %param.28) | copy-start | bytes 18436
  71.2 58.5 %copy-start.57 = (f32[2,768]{1,0:T(2,128)S(1)}, f32[2,768]{1,0:T(2,128)}, u32[]{:S(2)}) copy-start(f32[2,768]{1,0:T(2,128)} %param.31) | copy-start | bytes 18436
  71.2 58.5 %copy-start.58 = (f32[2,768]{1,0:T(2,128)S(1)}, f32[2,768]{1,0:T(2,128)}, u32[]{:S(2)}) copy-start(f32[2,768]{1,0:T(2,128)} %param.29) | copy-start | bytes 18436
  71.2 59.1 %copy-start.23 = (bf16[1,256,768]{2,1,0:T(8,128)(2,1)S(1)}, bf16[1,256,768]{2,1,0:T(8,128)(2,1)}, u32[]{:S(2)}) copy-start(bf16[1,256,768]{2,1,0:T(8,128)(2,1)} %param.17) | copy-start | bytes 1179652
  287.9 37.4 %copy-start.11 = (bf16[256,192]{1,0:T(8,128)(2,1)S(1)}, bf16[256,192]{1,0:T(8,128)(2,1)}, u32[]{:S(2)}) copy-start(bf16[256,192]{1,0:T(8,128)(2,1)} %copy-done.10) | copy-start | bytes 294916
  288.8 38.5 %copy-start.21 = (f32[256,768]{1,0:T(8,128)}, f32[256,768]{1,0:T(8,128)S(1)}, u32[]{:S(2)}) copy-start(f32[256,768]{1,0:T(8,128)S(1)} %get-tuple-element.72) | copy-start | bytes 2359300
  288.8 37.2 %copy-start.24 = (bf16[1,256,768]{2,1,0:T(8,128)(2,1)S(1)}, bf16[1,256,768]{2,1,0:T(8,128)(2,1)}, u32[]{:S(2)}) copy-start(bf16[1,256,768]{2,1,0:T(8,128)(2,1)} %param.17) | copy-start | bytes 1179652
  352.0 65.6 %copy-start.60 = (f32[256]{0:T(256)S(1)}, f32[256]{0:T(256)}, u32[]{:S(2)}) copy-start(f32[256]{0:T(256)} %get-tuple-element.44) | copy-start | bytes 3076
  352.0 65.6 %copy-start.59 = (f32[256]{0:T(256)S(1)}, f32[256]{0:T(256)}, u32[]{:S(2)}) copy-start(f32[256]{0:T(256)} %get-tuple-element.45) | copy-start | bytes 3076
  352.0 65.8 %copy-start.1 = (f32[256,768]{1,0:T(8,128)S(1)}, f32[256,768]{1,0:T(8,128)}, u32[]{:S(2)}) copy-start(f32[256,768]{1,0:T(8,128)} %copy-done) | copy-start | bytes 2359300
  352.0 65.8 %copy-start.22 = (f32[256,768]{1,0:T(8,128)S(1)}, f32[256,768]{1,0:T(8,128)}, u32[]{:S(2)}) copy-start(f32[256,768]{1,0:T(8,128)} %copy-done.21) | copy-start | bytes 2359300
  352.0 65.8 %copy-start.26 = (bf16[1,256,768]{2,1,0:T(8,128)(2,1)S(1)}, bf16[1,256,768]{2,1,0:T(8,128)(2,1)}, u32[]{:S(2)}) copy-start(bf16[1,256,768]{2,1,0:T(8,128)(2,1)} %param.17) | copy-start | bytes 1179652
  352.0 65.8 %copy-start.41 = (f32[256]{0:T(256)S(1)}, f32[256]{0:T(256)}, u32[]{:S(2)}) copy-start(f32[256]{0:T(256)} %copy-done.39) | copy-start | bytes 3076
  352.0 65.8 %copy-start.53 = (f32[256]{0:T(256)S(1)}, f32[256]{0:T(256)}, u32[]{:S(2)}) copy-start(f32[256]{0:T(256)} %copy-done.51) | copy-start | bytes 3076
  (44 other events, 750.9 us)
Sparse Core Ops, SparseCore 0:
  66.7 94.6 all-gather.1
  271.0 101.3 reduce-scatter.1
